TPU v7x, 128 devices: a whole 4x4x4 slice. The times are simulated.
128 devices in a mesh: section: 2 (over z_lo), ctx: 16 (over y, z_hi, core), tp: 4 (over x).
Axes of the slice: x: 4, y: 4, z: 4 (z_hi: 2, z_lo: 2; z = z_hi * 2 + z_lo), core: 2. Of those that a mesh axis runs over, the one named last changes fastest.
Arguments:
- frames: bfloat16 [4, 1, 1536, 768], P(None, None, 'ctx'), may hold values from -6 to 6
- w_qkv: bfloat16 [2, 768, 3, 768], P('section', 'ctx', None, 'tp'), may hold values from -0.21875 to 0.21875
- w_out: bfloat16 [2, 768, 768], P('section', 'tp', 'ctx'), may hold values from -0.21875 to 0.21875
- w_up: bfloat16 [2, 768, 3072], P('section', 'ctx', 'tp'), may hold values from -0.21875 to 0.21875
- w_down: bfloat16 [2, 3072, 768], P('section', 'tp', 'ctx'), may hold values from -0.109375 to 0.109375
- ln_gains: bfloat16 [2, 2, 768], P('section', None, 'ctx'), may hold values from 0.5 to 1.5
- shifts: bfloat16 [2, 4, 768], P('section', None, 'ctx'), may hold values from -3 to 3
- qv_bias: bfloat16 [2, 2, 768], P('section', None, ('tp', 'ctx')), may hold values from -3 to 3
- up_bias: bfloat16 [2, 3072], P('section', ('tp', 'ctx')), may hold values from -3 to 3
- lengths: int32 [4, 1], replicated, may hold values from 768 to 1536, as said below
- out_grad: bfloat16 [4, 1, 1536, 768], P(None, None, 'ctx'), may hold values from -6 to 6
Outputs:
- layer_outputs: float32 [2, 4, 1, 1536, 768], P('section', None, None, 'ctx')
- layer_input_grads: float32 [2, 4, 1, 1536, 768], P('section', None, None, 'ctx')
- grad_qkv: float32 [2, 768, 3, 768], P('section', 'ctx', None, 'tp')
- grad_out: float32 [2, 768, 768], P('section', 'tp', 'ctx')
- grad_up: float32 [2, 768, 3072], P('section', 'ctx', 'tp')
- grad_down: float32 [2, 3072, 768], P('section', 'tp', 'ctx')
- grad_gains: float32 [2, 2, 768], P('section', None, 'ctx')
- grad_shifts: float32 [2, 4, 768], P('section', None, 'ctx')
- grad_qv_bias: float32 [2, 2, 768], P('section', None, ('tp', 'ctx'))
- grad_up_bias: float32 [2, 3072], P('section', ('tp', 'ctx'))
Inputs may be any that keep to these rules, and one draw needn't show every extreme that they name: `lengths`: in micro-batch 0 one clip has all 1536 frames real.
All inputs are finite; a program needn't handle non-finite values.
Results may differ from a plain program's by a relative error of at most 0.04.
Values may be sent and summed in bfloat16 or wider, within the bound.
A program may use at most 192 MiB of HBM per device.

v0:
```python
import jax
import jax.numpy as jnp
from jax import lax
from jax.sharding import PartitionSpec as P

HEAD_DIM = 64


epsilon = 1e-05
negative = -1e30


def sent_together(arrays, axis, dim, along):
    ends, at = ([], 0)
    for a in arrays[:-1]:
        at += a.shape[along]
        ends.append(at)
    both = jnp.concatenate(arrays, axis=along)
    return tuple(jnp.split(lax.all_gather(both, axis, axis=dim, tiled=True), ends, axis=along))


def sent_to_all(array, axis):
    copies = jnp.broadcast_to(array, (lax.axis_size(axis), *array.shape))
    return lax.all_to_all(copies, axis, split_axis=0, concat_axis=0, tiled=True)


def of_everyone(array, axis):
    everything = sent_to_all(array, axis)
    return jnp.sum(everything.astype(jnp.float32), axis=0)


def side_by_side(arrays, axis, dim, along):
    ends, at = ([], 0)
    for a in arrays[:-1]:
        at += a.shape[along]
        ends.append(at)
    both = jnp.concatenate(arrays, axis=along)
    return tuple(
        jnp.split(lax.psum_scatter(both, axis, scatter_dimension=dim, tiled=True), ends, axis=along)
    )


def split_up(array, dim, size):
    before, after = (array.shape[:dim], array.shape[dim + 1 :])
    return jnp.moveaxis(array.reshape(*before, size, -1, *after), dim, 0)


def one_scatter(arrays, axis, dims):
    size = lax.axis_size(axis)
    pieces = [split_up(a, dim, size) for a, dim in zip(arrays, dims)]
    lines = jnp.concatenate([b.reshape(size, -1) for b in pieces], axis=1)
    extent = max(16, -(-lines.shape[1] // 1024) * 8)
    lines = jnp.pad(lines, ((0, 0), (0, extent * 128 - lines.shape[1]))).reshape(-1, 128)
    ravelled, at, done = (lax.psum_scatter(lines, axis, tiled=True).reshape(-1), 0, [])
    for b in pieces:
        part = b[0]
        done.append(ravelled[at : at + part.size].reshape(part.shape))
        at += part.size
    return tuple(done)


def passed_along(block, axis, distance):
    devices = range(lax.axis_size(axis))
    route = [(i - distance, i) for i in devices if i - distance in devices]
    return lax.ppermute(block, axis, route)


def normalize(values, norm_gain, norm_shift):
    center = values - jnp.mean(values, axis=-1, keepdims=True)
    spread = jnp.mean(center * center, axis=-1, keepdims=True)
    return center * lax.rsqrt(spread + epsilon) * norm_gain + norm_shift


def gelu_exact(values):
    return jax.nn.gelu(values, approximate=False)


def small_params(weights):
    return tuple((param.astype(jnp.float32) for param in weights[4:]))


def forward_layer(weights, layer_in, clip_lengths):
    w_qkv, w_out, w_up, w_down = weights[:4]
    gain_rows, shift_rows, qv_bias, up_bias = small_params(weights)
    clip_count, frame_count, model_width = layer_in.shape
    local_width = w_qkv.shape[2]
    head_count = local_width // HEAD_DIM
    scaling = HEAD_DIM ** (-0.5)
    layer_val = layer_in.astype(jnp.float32)
    normed = normalize(layer_val, gain_rows[0], shift_rows[0]).astype(jnp.bfloat16)
    projected = jnp.dot(
        normed.reshape(-1, model_width),
        w_qkv.reshape(model_width, 3 * local_width),
        preferred_element_type=jnp.float32,
    )
    projected = projected.reshape(clip_count, frame_count, 3, local_width)
    queries = (projected[:, :, 0] + qv_bias[0]).astype(jnp.bfloat16)
    key_rows = projected[:, :, 1].astype(jnp.bfloat16)
    value_rows = (projected[:, :, 2] + qv_bias[1]).astype(jnp.bfloat16)
    query_heads = queries.reshape(clip_count, frame_count, head_count, HEAD_DIM)
    start_top = jnp.full((clip_count, head_count, frame_count), negative, jnp.float32)
    keys_all, values_all = sent_together((key_rows, value_rows), "ctx", 1, 0)
    running_top = start_top
    extent = keys_all.shape[1]
    key_heads = keys_all.reshape(clip_count, extent, head_count, HEAD_DIM)
    value_heads = values_all.reshape(clip_count, extent, head_count, HEAD_DIM)
    scores = (
        jnp.einsum("cqhd,ckhd->chqk", query_heads, key_heads, preferred_element_type=jnp.float32)
        * scaling
    )
    usable = jnp.arange(extent, dtype=jnp.int32)[None, :] < clip_lengths[:, None]
    scores = jnp.where(usable[:, None, None, :], scores, negative)
    new_top = jnp.maximum(running_top, jnp.max(scores, axis=-1))
    softmax_w = jnp.exp(scores - new_top[..., None])
    totals = jnp.sum(softmax_w, axis=-1)
    update = jnp.einsum(
        "chqk,ckhd->chqd",
        softmax_w.astype(jnp.bfloat16),
        value_heads,
        preferred_element_type=jnp.float32,
    )
    running_top, totals, summed = (new_top, totals, update)
    stored = (keys_all, values_all)
    log_total = running_top + jnp.log(totals)
    attended = (
        (summed / totals[..., None])
        .transpose(0, 2, 1, 3)
        .reshape(clip_count, frame_count, local_width)
        .astype(jnp.bfloat16)
    )
    attn_part = jnp.dot(
        attended.reshape(-1, local_width), w_out, preferred_element_type=jnp.float32
    )
    attn_out = of_everyone(attn_part.astype(jnp.bfloat16), "tp").astype(jnp.float32) + shift_rows[2]
    middle = layer_val + attn_out.reshape(clip_count, frame_count, model_width)
    normed2 = normalize(middle, gain_rows[1], shift_rows[1]).astype(jnp.bfloat16)
    hidden_pre = (
        jnp.dot(normed2.reshape(-1, model_width), w_up, preferred_element_type=jnp.float32)
        + up_bias
    )
    activated = gelu_exact(hidden_pre).astype(jnp.bfloat16)
    down_part = jnp.dot(activated, w_down, preferred_element_type=jnp.float32)
    down_out = of_everyone(down_part.astype(jnp.bfloat16), "tp").astype(jnp.float32) + shift_rows[3]
    layer_out = middle + down_out.reshape(clip_count, frame_count, model_width)
    return (layer_out, middle, log_total, attended, stored)


def backward_layer(weights, layer_in, middle, log_total, attended, grad_out, clip_lengths, stored):
    w_qkv, w_out, w_up, w_down = weights[:4]
    gain_rows, shift_rows, qv_bias, up_bias = small_params(weights)
    clip_count, frame_count, model_width = layer_in.shape
    local_width = w_qkv.shape[2]
    head_count = local_width // HEAD_DIM
    scaling = HEAD_DIM ** (-0.5)
    layer_val = layer_in.astype(jnp.float32)
    normed_val, norm_back = jax.vjp(normalize, layer_val, gain_rows[0], shift_rows[0])
    normed = normed_val.astype(jnp.bfloat16).reshape(-1, model_width)
    projected = jnp.dot(
        normed, w_qkv.reshape(model_width, 3 * local_width), preferred_element_type=jnp.float32
    )
    projected = projected.reshape(clip_count, frame_count, 3, local_width)
    queries = (projected[:, :, 0] + qv_bias[0]).astype(jnp.bfloat16)
    query_heads = queries.reshape(clip_count, frame_count, head_count, HEAD_DIM)
    normed2_val, norm2_back = jax.vjp(normalize, middle, gain_rows[1], shift_rows[1])
    normed2 = normed2_val.astype(jnp.bfloat16).reshape(-1, model_width)
    hidden_pre = jnp.dot(normed2, w_up, preferred_element_type=jnp.float32) + up_bias
    activated_val, gelu_back = jax.vjp(gelu_exact, hidden_pre)
    activated = activated_val.astype(jnp.bfloat16)
    grad_down_in = grad_out.reshape(-1, model_width).astype(jnp.bfloat16)
    grad_down = jnp.dot(activated.T, grad_down_in, preferred_element_type=jnp.float32)
    grad_bias_down = jnp.sum(grad_down_in.astype(jnp.float32), axis=0)
    grad_act = jnp.dot(grad_down_in, w_down.T, preferred_element_type=jnp.float32)
    grad_pre = gelu_back(grad_act)[0].astype(jnp.bfloat16)
    grad_up = jnp.dot(normed2.T, grad_pre, preferred_element_type=jnp.float32)
    grad_up_bias = jnp.sum(grad_pre.astype(jnp.float32), axis=0)
    grad_norm2 = of_everyone(
        jnp.dot(grad_pre, w_up.T, preferred_element_type=jnp.float32).astype(jnp.bfloat16), "tp"
    ).astype(jnp.float32)
    grad_mid_norm, grad_gain2, grad_shift2 = norm2_back(
        grad_norm2.reshape(clip_count, frame_count, model_width)
    )
    grad_middle = grad_out + grad_mid_norm
    grad_attn = grad_middle.reshape(-1, model_width).astype(jnp.bfloat16)
    grad_out_proj = jnp.dot(
        attended.reshape(-1, local_width).T, grad_attn, preferred_element_type=jnp.float32
    )
    grad_bias_out = jnp.sum(grad_attn.astype(jnp.float32), axis=0)
    grad_att = jnp.dot(grad_attn, w_out.T, preferred_element_type=jnp.float32).astype(jnp.bfloat16)
    grad_att_heads = grad_att.reshape(clip_count, frame_count, head_count, HEAD_DIM)
    attended_heads = attended.reshape(clip_count, frame_count, head_count, HEAD_DIM)
    row_delta = jnp.sum(
        grad_att_heads.astype(jnp.float32) * attended_heads.astype(jnp.float32), axis=-1
    ).transpose(0, 2, 1)
    key_cur = stored[0]
    extent = key_cur.shape[1]
    key_heads = key_cur.reshape(clip_count, extent, head_count, HEAD_DIM)
    value_heads = stored[1].reshape(clip_count, extent, head_count, HEAD_DIM)
    scores = (
        jnp.einsum("cqhd,ckhd->chqk", query_heads, key_heads, preferred_element_type=jnp.float32)
        * scaling
    )
    usable = jnp.arange(extent, dtype=jnp.int32)[None, :] < clip_lengths[:, None]
    scores = jnp.where(usable[:, None, None, :], scores, negative)
    softmax_w = jnp.exp(scores - log_total[..., None])
    grad_probs = jnp.einsum(
        "cqhd,ckhd->chqk", grad_att_heads, value_heads, preferred_element_type=jnp.float32
    )
    grad_scores = (softmax_w * (grad_probs - row_delta[..., None])).astype(jnp.bfloat16)
    query_add = (
        jnp.einsum("chqk,ckhd->cqhd", grad_scores, key_heads, preferred_element_type=jnp.float32)
        * scaling
    )
    key_add = (
        jnp.einsum("chqk,cqhd->ckhd", grad_scores, query_heads, preferred_element_type=jnp.float32)
        * scaling
    )
    value_add = jnp.einsum(
        "chqk,cqhd->ckhd",
        softmax_w.astype(jnp.bfloat16),
        grad_att_heads,
        preferred_element_type=jnp.float32,
    )
    key_full = key_add.reshape(clip_count, extent, local_width)
    value_full = value_add.reshape(clip_count, extent, local_width)
    key_acc, value_acc = tuple(
        (
            part.astype(jnp.float32)
            for part in side_by_side(
                (key_full.astype(jnp.bfloat16), value_full.astype(jnp.bfloat16)), "ctx", 1, 0
            )
        )
    )
    grad_queries = query_add.reshape(clip_count, frame_count, local_width).astype(jnp.bfloat16)
    grad_keys = key_acc.astype(jnp.bfloat16)
    grad_values = value_acc.astype(jnp.bfloat16)
    grad_qv = jnp.stack(
        [
            jnp.sum(grad_queries.astype(jnp.float32), axis=(0, 1)),
            jnp.sum(grad_values.astype(jnp.float32), axis=(0, 1)),
        ]
    )
    grad_proj = jnp.stack([grad_queries, grad_keys, grad_values], axis=2).reshape(
        -1, 3 * local_width
    )
    grad_qkv = jnp.dot(normed.T, grad_proj, preferred_element_type=jnp.float32).reshape(
        model_width, 3, local_width
    )
    grad_norm1 = of_everyone(
        jnp.dot(
            grad_proj,
            w_qkv.reshape(model_width, 3 * local_width).T,
            preferred_element_type=jnp.float32,
        ).astype(jnp.bfloat16),
        "tp",
    ).astype(jnp.float32)
    grad_in_norm, grad_gain1, grad_shift1 = norm_back(
        grad_norm1.reshape(clip_count, frame_count, model_width)
    )
    grad_input = grad_middle + grad_in_norm
    grad_parts = (
        grad_qkv,
        grad_out_proj,
        grad_up,
        grad_down,
        jnp.stack([grad_gain1, grad_gain2]),
        jnp.stack([grad_shift1, grad_shift2, grad_bias_out, grad_bias_down]),
        grad_qv,
        grad_up_bias,
    )
    return (grad_input, grad_parts)


def add_parts(first_parts, other_parts):
    if first_parts is None:
        return other_parts
    return tuple(
        (left_part + right_part for left_part, right_part in zip(first_parts, other_parts))
    )


def scatter_parts(parts):
    return tuple(
        tuple(
            (
                part.astype(jnp.float32)
                for part in one_scatter(
                    (
                        parts[0].astype(jnp.bfloat16),
                        parts[1].astype(jnp.bfloat16),
                        parts[2].astype(jnp.bfloat16),
                        parts[3].astype(jnp.bfloat16),
                        parts[4].astype(jnp.bfloat16),
                        parts[5].astype(jnp.bfloat16),
                        parts[6].astype(jnp.bfloat16),
                        parts[7].astype(jnp.bfloat16),
                    ),
                    "ctx",
                    (0, 1, 0, 1, 1, 1, 1, 0),
                )
            )
        )
    )


def on_device(
    frames, w_qkv, w_out, w_up, w_down, ln_gains, shifts, qv_bias, up_bias, lengths, out_grad
):
    section_index = lax.axis_index("section")
    sections = lax.axis_size("section")
    batches = frames.shape[0]
    tick_count = batches + sections - 1
    held_weights = None
    held_weights = (
        lax.all_gather(w_qkv[0], "ctx", axis=0, tiled=True),
        lax.all_gather(w_out[0], "ctx", axis=1, tiled=True),
        lax.all_gather(w_up[0], "ctx", axis=0, tiled=True),
        *sent_together((w_down[0], ln_gains[0], shifts[0]), "ctx", 1, 0),
        lax.all_gather(qv_bias[0], "ctx", axis=1, tiled=True),
        lax.all_gather(up_bias[0], "ctx", axis=0, tiled=True),
    )
    incoming = jnp.zeros(frames.shape[1:], jnp.bfloat16)
    kept_in, kept_mid, kept_log, kept_att, kept_out, kept_keys, kept_values = (
        [],
        [],
        [],
        [],
        [],
        [],
        [],
    )
    for moment in range(tick_count):
        which_batch = jnp.clip(moment - section_index, 0, batches - 1)
        own_frames = lax.dynamic_index_in_dim(frames, which_batch, 0, keepdims=False)
        layer_in = jnp.where(section_index == 0, own_frames, incoming)
        clip_lengths = lax.dynamic_index_in_dim(lengths, which_batch, 0, keepdims=False)
        weights = held_weights
        layer_out, middle, log_total, attended, stored = forward_layer(
            weights, layer_in, clip_lengths
        )
        out_low = layer_out.astype(jnp.bfloat16)
        kept_in.append(layer_in)
        kept_mid.append(middle)
        kept_log.append(log_total)
        kept_att.append(attended)
        kept_out.append(layer_out)
        kept_keys.append(stored[0])
        kept_values.append(stored[1])
        if moment + 1 < tick_count:
            incoming = passed_along(out_low, "section", 1)
    outputs = lax.dynamic_slice_in_dim(jnp.stack(kept_out), section_index, batches, 0)
    stack_in = jnp.stack(kept_in)
    stack_mid = jnp.stack(kept_mid)
    stack_log = jnp.stack(kept_log)
    stack_att = jnp.stack(kept_att)
    stack_keys = jnp.stack(kept_keys)
    stack_values = jnp.stack(kept_values)
    returned = jnp.zeros(frames.shape[1:], jnp.float32)
    summed_parts = None
    input_grads = []
    for moment in range(tick_count):
        batch_pos = moment - (sections - 1 - section_index)
        usable = jnp.logical_and(batch_pos >= 0, batch_pos < batches)
        which_batch = jnp.clip(batch_pos, 0, batches - 1)
        stored_at = jnp.clip(batch_pos + section_index, 0, tick_count - 1)
        own_grad = lax.dynamic_index_in_dim(out_grad, which_batch, 0, keepdims=False).astype(
            jnp.float32
        )
        grad_out = jnp.where(section_index == sections - 1, own_grad, returned) * usable.astype(
            jnp.float32
        )
        layer_in = lax.dynamic_index_in_dim(stack_in, stored_at, 0, keepdims=False)
        middle = lax.dynamic_index_in_dim(stack_mid, stored_at, 0, keepdims=False)
        log_total = lax.dynamic_index_in_dim(stack_log, stored_at, 0, keepdims=False)
        attended = lax.dynamic_index_in_dim(stack_att, stored_at, 0, keepdims=False)
        clip_lengths = lax.dynamic_index_in_dim(lengths, which_batch, 0, keepdims=False)
        stored = (
            lax.dynamic_index_in_dim(stack_keys, stored_at, 0, keepdims=False),
            lax.dynamic_index_in_dim(stack_values, stored_at, 0, keepdims=False),
        )
        weights = held_weights
        grad_input, grad_parts = backward_layer(
            weights, layer_in, middle, log_total, attended, grad_out, clip_lengths, stored
        )
        input_grads.append(grad_input)
        summed_parts = add_parts(summed_parts, grad_parts)
        if moment + 1 < tick_count:
            returned = passed_along(grad_input.astype(jnp.bfloat16), "section", -1).astype(
                jnp.float32
            )
    summed_parts = scatter_parts(summed_parts)
    grads_in = lax.dynamic_slice_in_dim(
        jnp.stack(input_grads), sections - 1 - section_index, batches, 0
    )
    return (
        outputs[None],
        grads_in[None],
        summed_parts[0][None],
        summed_parts[1][None],
        summed_parts[2][None],
        summed_parts[3][None],
        summed_parts[4][None],
        summed_parts[5][None],
        summed_parts[6][None],
        summed_parts[7][None],
    )


def solution(mesh):
    in_specs = (
        P(None, None, "ctx", None),
        P("section", "ctx", None, "tp"),
        P("section", "tp", "ctx"),
        P("section", "ctx", "tp"),
        P("section", "tp", "ctx"),
        P("section", None, "ctx"),
        P("section", None, "ctx"),
        P("section", None, ("tp", "ctx")),
        P("section", ("tp", "ctx")),
        P(),
        P(None, None, "ctx", None),
    )
    out_specs = (
        P("section", None, None, "ctx", None),
        P("section", None, None, "ctx", None),
        P("section", "ctx", None, "tp"),
        P("section", "tp", "ctx"),
        P("section", "ctx", "tp"),
        P("section", "tp", "ctx"),
        P("section", None, "ctx"),
        P("section", None, "ctx"),
        P("section", None, ("tp", "ctx")),
        P("section", ("tp", "ctx")),
    )
    return jax.shard_map(
        on_device, mesh=mesh, in_specs=in_specs, out_specs=out_specs, check_vma=False
    )
```

profile of v0, /device:TPU:1, one launch (start us, length us, event | category | flops | bytes accessed | tf_op | source)
XLA Modules:
  0.0 1499.0 jit_solution(14544457813767715716)
XLA Ops:
  10.5 30.6 %all-gather = bf16[1,768,3,192]{3,1,2,0:T(8,128)(2,1)S(1)} all-gather(bf16[1,48,3,192]{3,1,2,0:T(8,128)(2,1)} %param.12), channel_id=2, replica_groups=mesh['section'=2,'ctx'=16,'tp'=4] {'ctx'}, dimensions={1}, use_global_device_ids=true | all-gather | bytes 940032 | tf_op jit(solution)/shard_map/all_gather | solution.py:314
  41.9 20.2 %all-gather.1 = bf16[1,2,192]{1,0,2:T(2,128)(2,1)S(1)} all-gather(bf16[1,2,12]{1,0,2:T(2,128)(2,1)S(1)} %copy.218), channel_id=3, replica_groups=mesh['section'=2,'ctx'=16,'tp'=4] {'ctx'}, dimensions={2}, use_global_device_ids=true | all-gather | bytes 816 | tf_op jit(solution)/shard_map/all_gather | solution.py:318
  72.1 22.6 %all-gather.2 = bf16[1,192,768]{1,2,0:T(8,128)(2,1)S(1)} all-gather(bf16[1,192,48]{1,2,0:T(8,128)(2,1)S(1)} %copy-done.234), channel_id=4, replica_groups=mesh['section'=2,'ctx'=16,'tp'=4] {'ctx'}, dimensions={2}, use_global_device_ids=true | all-gather | bytes 313344 | tf_op jit(solution)/shard_map/all_gather | solution.py:315
  94.9 20.6 %all-gather.15.cloned.1.call-done = bf16[2,1536,192]{2,1,0:T(8,128)(2,1)} async-done(((bf16[2,96,192]{2,1,0:T(8,128)(2,1)}), bf16[2,1536,192]{2,1,0:T(8,128)(2,1)}) %all-gather.15.cloned.1.call-update) | async-done | bytes 1179664 | tf_op jit(solution)/shard_map/all_gather | solution.py:19
  129.1 33.1 %all-reduce.1 = bf16[768]{0:T(1024)(128)(2,1)S(1)} all-reduce(bf16[768]{0:T(1024)(128)(2,1)S(1)} %dynamic-update-slice), channel_id=6, replica_groups=mesh['section'=2,'ctx'=16,'tp'=4] {'ctx'}, use_global_device_ids=true, to_apply=%add.1 | all-reduce | flops 768 | bytes 3072
  165.6 12.0 all_to_all.100
  185.4 48.0 %all-gather.17.cloned.1.call-done = bf16[2,1536,192]{2,1,0:T(8,128)(2,1)} async-done(((bf16[2,96,192]{2,1,0:T(8,128)(2,1)}), bf16[2,1536,192]{2,1,0:T(8,128)(2,1)}) %all-gather.17.cloned.1.call-update) | async-done | bytes 1179664 | tf_op jit(solution)/shard_map/all_gather | solution.py:19
  247.2 8.0 all-to-all-done.2
  266.8 11.4 all_to_all.101
  291.3 43.9 %all-gather.19.cloned.1.call-done = bf16[2,1536,192]{2,1,0:T(8,128)(2,1)} async-done(((bf16[2,96,192]{2,1,0:T(8,128)(2,1)}), bf16[2,1536,192]{2,1,0:T(8,128)(2,1)}) %all-gather.19.cloned.1.call-update) | async-done | bytes 1179664 | tf_op jit(solution)/shard_map/all_gather | solution.py:19
  345.9 13.4 all_to_all.102
  369.0 11.1 all_to_all.103
  403.6 33.8 %all-gather.21.cloned.1.call-done = bf16[2,1536,192]{2,1,0:T(8,128)(2,1)} async-done(((bf16[2,96,192]{2,1,0:T(8,128)(2,1)}), bf16[2,1536,192]{2,1,0:T(8,128)(2,1)}) %all-gather.21.cloned.1.call-update) | async-done | bytes 1179664 | tf_op jit(solution)/shard_map/all_gather | solution.py:19
  457.1 5.9 all-to-all-done.6
  482.3 6.1 all-to-all-done.7
  513.9 33.9 %all-gather.23.cloned.1.call-done = bf16[2,1536,192]{2,1,0:T(8,128)(2,1)} async-done(((bf16[2,96,192]{2,1,0:T(8,128)(2,1)}), bf16[2,1536,192]{2,1,0:T(8,128)(2,1)}) %all-gather.23.cloned.1.call-update) | async-done | bytes 1179664 | tf_op jit(solution)/shard_map/all_gather | solution.py:19
  614.2 4.8 copy.266
  638.5 50.3 %reduce-scatter.16.cloned.1.call-done = bf16[96,384]{1,0:T(8,128)(2,1)} async-done(((bf16[1536,384]{1,0:T(8,128)(2,1)}), bf16[96,384]{1,0:T(8,128)(2,1)}) %reduce-scatter.16.cloned.1.call-update) | async-done | bytes 73744
  704.1 5.0 all-to-all-done.11
  800.1 32.8 %reduce-scatter.18.cloned.1.call-done = bf16[96,384]{1,0:T(8,128)(2,1)} async-done(((bf16[1536,384]{1,0:T(8,128)(2,1)}), bf16[96,384]{1,0:T(8,128)(2,1)}) %reduce-scatter.18.cloned.1.call-update) | async-done | bytes 73744
  875.9 5.0 all-to-all-done.14
  897.2 4.9 copy.270
  928.7 46.4 %reduce-scatter.20.cloned.1.call-done = bf16[96,384]{1,0:T(8,128)(2,1)} async-done(((bf16[1536,384]{1,0:T(8,128)(2,1)}), bf16[96,384]{1,0:T(8,128)(2,1)}) %reduce-scatter.20.cloned.1.call-update) | async-done | bytes 73744
  1049.6 4.8 copy.272
  1084.2 43.7 %reduce-scatter.22.cloned.1.call-done = bf16[96,384]{1,0:T(8,128)(2,1)} async-done(((bf16[1536,384]{1,0:T(8,128)(2,1)}), bf16[96,384]{1,0:T(8,128)(2,1)}) %reduce-scatter.22.cloned.1.call-update) | async-done | bytes 73744
  1207.9 4.9 copy.274
  1217.3 5.6 add_convert_fusion.1
  1225.3 6.1 add_convert_fusion
  1235.4 8.3 reshape.7962
  1267.3 20.2 %reduce-scatter.24.cloned.1.call-done = bf16[96,384]{1,0:T(8,128)(2,1)} async-done(((bf16[1536,384]{1,0:T(8,128)(2,1)}), bf16[96,384]{1,0:T(8,128)(2,1)}) %reduce-scatter.24.cloned.1.call-update) | async-done | bytes 73744
  1343.1 6.1 all-to-all-done.9
  1360.4 122.1 %all-reduce.5.cloned.1.call-done = bf16[13952,128]{1,0:T(8,128)(2,1)} async-done(((bf16[13952,128]{1,0:T(8,128)(2,1)}), bf16[13952,128]{1,0:T(8,128)(2,1)}) %all-reduce.5.cloned.1.call-update) | async-done | bytes 3571728
  (1223 shorter events, 753.5 us)
Async XLA Ops:
  7.2 58.4 %all-gather.13.cloned.1.call-start = ((), (), s32[]{:S(2)}) async-start(), calls=%async_computation.25 | async-start | bytes 1462272 | tf_op jit(solution)/shard_map/all_gather | solution.py:19
  10.4 105.1 %all-gather.15.cloned.1.call-start = ((), (), s32[]{:S(2)}) async-start(), calls=%async_computation.26 | async-start | bytes 1671168 | tf_op jit(solution)/shard_map/all_gather | solution.py:19
  69.9 92.7 %all-gather.25.cloned.1.call-start = ((), (), s32[]{:S(2)}) async-start(), calls=%async_computation.31 | async-start | bytes 1253376 | tf_op jit(solution)/shard_map/all_gather | solution.py:316
  123.5 38.6 %all-to-all-start = ((bf16[4,96,768]{2,1,0:T(8,128)(2,1)}), bf16[4,96,768]{2,1,0:T(8,128)(2,1)S(1)}, u32[]{:S(2)}, u32[]{:S(2)}) async-start(bf16[4,96,768]{2,1,0:T(8,128)(2,1)} %broadcast_in_dim.174), calls=%async_computation | async-start | bytes 1179648 | tf_op jit(solution)/shard_map/all_to_all | solution.py:24
  127.5 106.0 %all-gather.17.cloned.1.call-start = ((), (), s32[]{:S(2)}) async-start(), calls=%async_computation.27 | async-start | bytes 1671168 | tf_op jit(solution)/shard_map/all_gather | solution.py:19
  241.0 14.1 all-to-all-start.2
  245.2 90.0 %all-gather.19.cloned.1.call-start = ((), (), s32[]{:S(2)}) async-start(), calls=%async_computation.28 | async-start | bytes 1671168 | tf_op jit(solution)/shard_map/all_gather | solution.py:19
  286.9 150.5 %all-gather.21.cloned.1.call-start = ((), (), s32[]{:S(2)}) async-start(), calls=%async_computation.29 | async-start | bytes 1671168 | tf_op jit(solution)/shard_map/all_gather | solution.py:19
  448.9 14.1 all-to-all-start.6
  475.4 12.9 all-to-all-start.7
  479.6 68.2 %all-gather.23.cloned.1.call-start = ((), (), s32[]{:S(2)}) async-start(), calls=%async_computation.30 | async-start | bytes 1671168 | tf_op jit(solution)/shard_map/all_gather | solution.py:19
  559.3 14.1 all-to-all-start.8
  583.0 14.7 all-to-all-start.10
  587.2 101.5 %reduce-scatter.16.cloned.1.call-start = ((), (), s32[]{:S(2)}) async-start(), calls=%async_computation.32 | async-start | bytes 1253376
  697.5 11.5 all-to-all-start.11
  715.4 5.9 collective-permute-start.4
  725.5 12.8 all-to-all-start.12
  729.6 103.2 %reduce-scatter.18.cloned.1.call-start = ((), (), s32[]{:S(2)}) async-start(), calls=%async_computation.33 | async-start | bytes 1253376
  841.6 11.5 all-to-all-start.13
  869.4 11.5 all-to-all-start.14
  873.6 101.5 %reduce-scatter.20.cloned.1.call-start = ((), (), s32[]{:S(2)}) async-start(), calls=%async_computation.34 | async-start | bytes 1253376
  983.8 13.1 all-to-all-start.15
  1002.0 6.0 collective-permute-start.6
  1013.2 20.1 %all-to-all-start.16 = ((bf16[4,96,768]{2,1,0:T(8,128)(2,1)}), bf16[4,96,768]{2,1,0:T(8,128)(2,1)}, u32[]{:S(2)}, u32[]{:S(2)}) async-start(bf16[4,96,768]{2,1,0:T(8,128)(2,1)} %broadcast_in_dim.389), calls=%async_computation.16 | async-start | bytes 1179648 | tf_op jit(solution)/shard_map/all_to_all | solution.py:24
  1017.4 110.5 %reduce-scatter.22.cloned.1.call-start = ((), (), s32[]{:S(2)}) async-start(), calls=%async_computation.35 | async-start | bytes 1253376
  1136.7 11.5 all-to-all-start.17
  1154.1 14.8 collective-permute-start.7
  1175.5 15.9 %all-to-all-start.18 = ((bf16[4,96,768]{2,1,0:T(8,128)(2,1)}), bf16[4,96,768]{2,1,0:T(8,128)(2,1)}, u32[]{:S(2)}, u32[]{:S(2)}) async-start(bf16[4,96,768]{2,1,0:T(8,128)(2,1)} %broadcast_in_dim.396), calls=%async_computation.18 | async-start | bytes 1179648 | tf_op jit(solution)/shard_map/all_to_all | solution.py:24
  1179.7 107.8 %reduce-scatter.24.cloned.1.call-start = ((), (), s32[]{:S(2)}) async-start(), calls=%async_computation.36 | async-start | bytes 1253376
  1296.3 17.9 %all-to-all-start.19 = ((bf16[4,96,768]{2,1,0:T(8,128)(2,1)}), bf16[4,96,768]{2,1,0:T(8,128)(2,1)}, u32[]{:S(2)}, u32[]{:S(2)}) async-start(bf16[4,96,768]{2,1,0:T(8,128)(2,1)} %broadcast_in_dim.400), calls=%async_computation.19 | async-start | bytes 1179648 | tf_op jit(solution)/shard_map/all_to_all | solution.py:24
  1300.5 182.0 %all-reduce.5.cloned.1.call-start = ((), (), s32[]{:S(2)}) async-start(), calls=%async_computation.37 | async-start | bytes 7143424
  1337.4 11.8 all-to-all-start.9
  (312 other events, 1887.4 us)
Sparse Core Ops, SparseCore 0:
  10.9 51.3 all-gather.12
  70.1 45.3 all-gather.14
  117.9 44.3 all-gather.24
  184.1 49.2 all-gather.16
  287.0 48.1 all-gather.18
  388.8 48.5 all-gather.20
  499.3 48.4 all-gather.22
  623.6 65.0 reduce-scatter.15
  763.3 69.4 reduce-scatter.17
  906.7 68.3 reduce-scatter.19
  1059.0 68.8 reduce-scatter.21
  1217.4 70.0 reduce-scatter.23
  1331.5 150.9 all-reduce.4
where the time goes:
time: 1520 us; the launch traced here: 1500 us
  waiting for transfers between devices  556 us (37%)
  local copies, waits for them, and re-layouts  352 us (23%)
  other arithmetic  173 us (11%)
  matrix products  161 us (11%)
  blocking collectives  154 us (10%)
  starting transfers between devices  82.6 us (5%)
  between operations  20.1 us (1%)
    unnamed x19, waiting for transfers between devices  316 us
    all_gather x6, waiting for transfers between devices, sent_together(): lax.all_gather(both, axis, axis=dim, tiled=True)  180 us
    unnamed x661, local copies, waits for them, and re-layouts  121 us
    all_to_all x16, starting transfers between devices, sent_to_all(): return lax.all_to_all(copies, axis, split_axis=0, concat_axis=0, tiled=True)  66.3 us
    all_to_all x4, blocking collectives, sent_to_all(): return lax.all_to_all(copies, axis, split_axis=0, concat_axis=0, tiled=True)  47.8 us
    all_to_all x16, waiting for transfers between devices, sent_to_all(): return lax.all_to_all(copies, axis, split_axis=0, concat_axis=0, tiled=True)  43.8 us
    reduce_sum x24, other arithmetic, normalize(): return center * lax.rsqrt(spread + epsilon) * norm_gain + norm_shift  34.6 us
    unnamed x1, blocking collectives  33.1 us
  transfers between devices with their start and end apart: 37, of which 26 were waited for; matrix products, arithmetic and copies ran while one was open for 22% of the time, Pallas kernels for 0%

commit v1 on v0

v1 whole, which is shorter than its diff:
```python
import functools

import jax
import jax.numpy as jnp
import numpy as np
from jax import lax
from jax.experimental import pallas as pl
from jax.experimental.pallas import tpu as pltpu
from jax.sharding import PartitionSpec as P

MESH = pl.DeviceIdType.MESH
f32 = jnp.float32
bf16 = jnp.bfloat16
epsilon = 1e-05
negative = -1e30

D = 768
SHARD = 48
QUARTER = 48
BLOCK = 96
ROWS = 192
KEYS = 1536
Q0, KV0, OUT0, UP0, DOWN0, WIDE = 0, 256, 640, 896, 1664, 2432
HALF = 1280
PIECE = 256
HEADS3 = 3
VMEM_LIMIT = 60 * 1024 * 1024


def where_am_i():
    s = lax.axis_index("section")
    c = lax.axis_index("ctx")
    t = lax.axis_index("tp")
    y = lax.div(c, 4)
    zh = lax.rem(lax.div(c, 2), 2)
    core = lax.rem(c, 2)
    return y, zh * 2 + s, core, t


def ident(y, z, core, t):
    return {"section": lax.rem(z, 2), "ctx": y * 4 + lax.div(z, 2) * 2 + core, "tp": t}


def ring(i, d):
    return lax.rem(i + d, 4)


def greet(peers):
    barrier = pltpu.get_barrier_semaphore()
    for peer in peers:
        pl.semaphore_signal(barrier, inc=1, device_id=peer, device_id_type=MESH)
    pl.semaphore_wait(barrier, len(peers))


def remote(src, dst, send, recv, peer):
    return pltpu.make_async_remote_copy(
        src_ref=src, dst_ref=dst, send_sem=send, recv_sem=recv, device_id=peer, device_id_type=MESH
    )


def gather_kernel(w_ref, f_ref, g_ref, w_all, x_all, g_all, send, recv, local):
    y, z, core, t = where_am_i()
    other = 1 - core

    def spot(da, db):
        return ring(y, da * core + db * other), ring(z, da * other + db * core)

    def peer(da, db):
        yy, zz = spot(da, db)
        return ident(yy, zz, core, t)

    def block(da, db, of_core, half=None):
        yy, zz = spot(da, db)
        row = pl.multiple_of((yy * 4 + lax.div(zz, 2) * 2 + of_core) * SHARD, SHARD)
        cols = {None: pl.ds(0, WIDE), 0: pl.ds(0, HALF), 1: pl.ds(HALF, WIDE - HALF)}[half]
        return w_all.at[lax.rem(zz, 2), pl.ds(row, SHARD), cols]

    zh = lax.div(z, 2)
    twin = ident(y, 3 - z, core, t)
    mate = ident(y, z, other, t)
    greet([peer(1, 0), peer(3, 0), peer(0, 1), peer(0, 3), mate])

    sent = []

    def put(k, src, dst, to):
        copy = remote(src, dst, send.at[k], recv.at[k], to)
        copy.start()
        sent.append(copy)

    def got(k, region):
        remote(region, region, send.at[k], recv.at[k], mate).wait_recv()

    own = block(0, 0, core)
    put(0, w_ref, own, peer(1, 0))
    put(1, w_ref, own, peer(3, 0))
    put(4, w_ref, own, peer(0, 1))
    put(5, w_ref, own, peer(0, 3))
    put(20, w_ref, own, mate)
    mine = pl.ds(pl.multiple_of(zh * BLOCK, BLOCK), BLOCK)
    theirs = pl.ds(pl.multiple_of((1 - zh) * BLOCK, BLOCK), BLOCK)
    put(36, f_ref.at[3 - z], x_all.at[mine], twin)
    put(37, g_ref.at[3 - z], g_all.at[mine], twin)
    kept = [
        pltpu.make_async_copy(w_ref, own, local.at[0]),
        pltpu.make_async_copy(f_ref.at[z], x_all.at[mine], local.at[1]),
        pltpu.make_async_copy(g_ref.at[z], g_all.at[mine], local.at[2]),
    ]
    for copy in kept:
        copy.start()

    def spread(j, da):
        put(4 + 4 * j, block(da, 0, core), block(da, 0, core), peer(0, 1))
        put(5 + 4 * j, block(da, 0, core), block(da, 0, core), peer(0, 3))
        put(20 + 4 * j, block(da, 0, core), block(da, 0, core), mate)

    got(0, block(3, 0, core))
    put(2, block(3, 0, core, 0), block(3, 0, core, 0), peer(1, 0))
    spread(1, 3)
    got(1, block(1, 0, core))
    put(3, block(1, 0, core, 1), block(1, 0, core, 1), peer(3, 0))
    spread(2, 1)

    def second(j, da):
        k = 4 + 4 * j
        got(k, block(da, 3, core))
        put(k + 2, block(da, 3, core, 0), block(da, 3, core, 0), peer(0, 1))
        put(20 + 4 * j + 1, block(da, 3, core), block(da, 3, core), mate)
        got(k + 1, block(da, 1, core))
        put(k + 3, block(da, 1, core, 1), block(da, 1, core, 1), peer(0, 3))
        put(20 + 4 * j + 2, block(da, 1, core), block(da, 1, core), mate)

    def last(j, da):
        k = 4 + 4 * j
        got(k + 2, block(da, 2, core, 0))
        got(k + 3, block(da, 2, core, 1))
        put(20 + 4 * j + 3, block(da, 2, core), block(da, 2, core), mate)

    second(0, 0)
    got(2, block(2, 0, core, 0))
    got(3, block(2, 0, core, 1))
    spread(3, 2)
    second(1, 3)
    last(0, 0)
    second(2, 1)
    last(1, 3)
    second(3, 2)
    last(2, 1)
    last(3, 2)
    for k in range(16):
        got(20 + k, own)
    got(36, x_all.at[theirs])
    got(37, g_all.at[theirs])
    for copy in kept:
        copy.wait()
    for copy in sent:
        copy.wait_send()


def gather_call(w, frames, out_grad):
    anywhere = pl.BlockSpec(memory_space=pl.ANY)
    return pl.pallas_call(
        gather_kernel,
        out_shape=(
            jax.ShapeDtypeStruct((2, D, WIDE), bf16),
            jax.ShapeDtypeStruct((ROWS, D), bf16),
            jax.ShapeDtypeStruct((ROWS, D), bf16),
        ),
        in_specs=[anywhere] * 3,
        out_specs=(anywhere,) * 3,
        scratch_shapes=[
            pltpu.SemaphoreType.DMA((38,)),
            pltpu.SemaphoreType.DMA((38,)),
            pltpu.SemaphoreType.DMA((3,)),
        ],
        compiler_params=pltpu.CompilerParams(collective_id=0, has_side_effects=True),
        name="weights_to_all",
    )(w, frames, out_grad)


def dot(a, b):
    return lax.dot_general(a, b, (((1,), (0,)), ((), ())), preferred_element_type=f32)


def dot_t(a, b):
    return lax.dot_general(a, b, (((1,), (1,)), ((), ())), preferred_element_type=f32)


def hat(v):
    center = v - jnp.mean(v, axis=-1, keepdims=True)
    r = lax.rsqrt(jnp.mean(center * center, axis=-1, keepdims=True) + epsilon)
    return center * r, r


def norm(v, gain, shift):
    return hat(v)[0] * gain + shift


def norm_back(v, gain, c):
    vhat, r = hat(v)
    cg = c * gain
    grad = r * (
        cg - jnp.mean(cg, axis=-1, keepdims=True) - vhat * jnp.mean(cg * vhat, axis=-1, keepdims=True)
    )
    return grad, jnp.sum(c * vhat, axis=0, keepdims=True), jnp.sum(c, axis=0, keepdims=True)


def layers_kernel(
    w_hbm, x_ref, g_ref, keep_ref, sel_ref,
    kept_ref, grads_ref,
    w_ref, w_sem, n1, n2, gdi0, ga, rs, part, kv, att, act, slope, mid, lse, q, small, scores, acc,
    dkv, dqkv, core_in, step_out, step1, step2, little,
    x_send, x_recv, k_send, k_recv,
):
    y, z, core, t = where_am_i()
    other = 1 - core
    mate = ident(y, z, other, t)
    up_peer = ident(ring(y, 1), z, core, t)
    down_peer = ident(ring(y, 3), z, core, t)
    loads = [pltpu.make_async_copy(w_hbm.at[l], w_ref.at[l], w_sem.at[l]) for l in range(2)]
    for load in loads:
        load.start()
    greet([ident(y, z, core, ring(t, d)) for d in (1, 2, 3)] + [up_peer, down_peer, mate])
    sent = []
    quarter = pl.ds(pl.multiple_of(t * QUARTER, QUARTER), QUARTER)

    def put(src, dst, send, recv, to):
        copy = remote(src, dst, send, recv, to)
        copy.start()
        sent.append(copy)

    def got(region, send, recv):
        remote(region, region, send, recv, mate).wait_recv()

    def rows_of(i):
        return pl.ds(pl.multiple_of(i * QUARTER, QUARTER), QUARTER)

    def share_start(phase, ref):
        for d in (1, 2, 3):
            put(ref.at[quarter], ref.at[quarter], x_send.at[phase, d - 1], x_recv.at[phase, d - 1],
                ident(y, z, core, ring(t, d)))

    def share_wait(phase, ref):
        for d in (1, 2, 3):
            got(ref.at[rows_of(ring(t, 4 - d))], x_send.at[phase, d - 1], x_recv.at[phase, d - 1])

    def sum_start(phase, i):
        for d in (1, 2, 3):
            put(part.at[i, rows_of(ring(t, d))], rs.at[i, d - 1], x_send.at[phase, d - 1],
                x_recv.at[phase, d - 1], ident(y, z, core, ring(t, d)))

    def sum_wait(phase, i):
        total = part[i, quarter, :].astype(f32)
        for d in (1, 2, 3):
            got(rs.at[i, d - 1], x_send.at[phase, d - 1], x_recv.at[phase, d - 1])
            total = total + rs[i, d - 1].astype(f32)
        return total

    col = lax.broadcasted_iota(jnp.int32, (1, 256), 1)
    q_masks = [jnp.where((col >= 64 * h) & (col < 64 * h + 64), 1.0, 0.0).astype(f32) for h in range(3)]
    v_masks = [jnp.where((col >= 64 * h + 64) & (col < 64 * h + 128), 1.0, 0.0).astype(f32) for h in range(3)]

    def by_head(rows, masks):
        rows = rows.astype(f32)
        return jnp.concatenate([rows * m for m in masks], axis=0)

    def from_heads(rows, masks):
        return sum(rows[h * ROWS : (h + 1) * ROWS] * masks[h] for h in range(3))

    def kv_rows(yy, of_core, first=0, size=ROWS):
        return pl.ds(pl.multiple_of((yy * 2 + of_core) * ROWS + first, BLOCK), size)

    def load_small(l):
        loads[l].wait()
        tile = w_ref[l, :, OUT0 : OUT0 + 128].astype(f32).T
        small[l] = tile[:16]

    def kv_share(l):
        buf = kv.at[l]
        s, r = k_send.at[l], k_recv.at[l]
        own = buf.at[kv_rows(y, core)]
        put(own, own, s.at[0], r.at[0], up_peer)
        put(own, own, s.at[1], r.at[1], down_peer)
        put(own, own, s.at[4], r.at[4], mate)
        before, after, across = ring(y, 3), ring(y, 1), ring(y, 2)
        whole = buf.at[kv_rows(before, core)]
        got(whole, s.at[0], r.at[0])
        first = buf.at[kv_rows(before, core, 0, BLOCK)]
        put(first, first, s.at[2], r.at[2], up_peer)
        put(whole, whole, s.at[5], r.at[5], mate)
        whole = buf.at[kv_rows(after, core)]
        got(whole, s.at[1], r.at[1])
        second = buf.at[kv_rows(after, core, BLOCK, BLOCK)]
        put(second, second, s.at[3], r.at[3], down_peer)
        put(whole, whole, s.at[6], r.at[6], mate)
        for i, k in ((0, 2), (1, 3)):
            piece = buf.at[kv_rows(across, core, i * BLOCK, BLOCK)]
            got(piece, s.at[k], r.at[k])
            put(piece, piece, s.at[7 + i], r.at[7 + i], mate)
        got(buf.at[kv_rows(y, other)], s.at[4], r.at[4])
        got(buf.at[kv_rows(before, other)], s.at[5], r.at[5])
        got(buf.at[kv_rows(after, other)], s.at[6], r.at[6])
        got(buf.at[kv_rows(across, other, 0, BLOCK)], s.at[7], r.at[7])
        got(buf.at[kv_rows(across, other, BLOCK, BLOCK)], s.at[8], r.at[8])

    def attend(l):
        q3 = by_head(q[l], q_masks).astype(bf16)

        def first(i, top):
            at = pl.ds(pl.multiple_of(i * PIECE, PIECE), PIECE)
            s = dot_t(kv[l, at, 0:256], q3)
            s = jnp.where(keep_ref[at, :] < 0, negative, s)
            scores[at, :] = s
            return jnp.maximum(top, jnp.max(s, axis=0, keepdims=True))

        top = lax.fori_loop(0, KEYS // PIECE, first, jnp.full((1, 3 * ROWS), negative, f32))
        acc[...] = jnp.zeros_like(acc)

        def second(i, total):
            at = pl.ds(pl.multiple_of(i * PIECE, PIECE), PIECE)
            p = jnp.exp(scores[at, :] - top)
            acc[...] += dot(kv[l, at, 128:384].T, p.astype(bf16))
            return total + jnp.sum(p, axis=0, keepdims=True)

        total = lax.fori_loop(0, KEYS // PIECE, second, jnp.zeros((1, 3 * ROWS), f32))
        lse[l] = top + jnp.log(total)
        att[l] = from_heads((acc[...] / total).T, v_masks).astype(bf16)

    def forward(l, x_q):
        row = small[l]
        bias = dot(row.astype(bf16), sel_ref[...])
        wide = dot(n1[l], w_ref[l, :, Q0:OUT0])
        q[l] = ((wide[:, :256] + bias[7:8, :256]).astype(bf16).astype(f32) * 0.125).astype(bf16)
        kv[l, kv_rows(y, core), :] = (wide[:, 256:] + bias[8:9, 256:]).astype(bf16)
        kv_share(l)
        attend(l)
        part[2 * l] = dot_t(att[l], w_ref[l, :, OUT0:UP0]).astype(bf16)
        sum_start(4 * l, 2 * l)
        m = x_q + sum_wait(4 * l, 2 * l) + row[4:5]
        mid[l] = m
        n2[l, quarter, :] = norm(m, row[1:2], row[3:4]).astype(bf16)
        share_start(4 * l + 1, n2.at[l])
        share_wait(4 * l + 1, n2.at[l])
        u = dot(n2[l], w_ref[l, :, UP0:DOWN0]) + row[6:7]
        phi = 0.5 * (1.0 + lax.erf(u * np.float32(0.5**0.5)))
        act[l] = (u * phi).astype(bf16)
        part[2 * l + 1] = dot_t(act[l], w_ref[l, :, DOWN0:WIDE]).astype(bf16)
        sum_start(4 * l + 2, 2 * l + 1)
        slope[l] = phi + u * jnp.exp(-0.5 * u * u) * np.float32((2 * np.pi) ** -0.5)
        out = m + sum_wait(4 * l + 2, 2 * l + 1) + row[5:6]
        kept_ref[l, 0] = out.astype(bf16)
        return out

    def dkv_sum(l):
        s, r = k_send.at[2 + l], k_recv.at[2 + l]
        for i in range(4):
            put(dkv.at[l, kv_rows(i, other)], core_in.at[l, i], s.at[i], r.at[i], mate)

        def mine(yy):
            return dkv[l, kv_rows(yy, core), :].astype(f32) + core_in[l, yy].astype(f32)

        for i in range(4):
            got(core_in.at[l, i], s.at[i], r.at[i])
        before, after, across = ring(y, 3), ring(y, 1), ring(y, 2)
        step_out[l, 0] = mine(across).astype(bf16)
        put(step_out.at[l, 0, pl.ds(0, BLOCK)], step1.at[l, 0], s.at[4], r.at[4], up_peer)
        put(step_out.at[l, 0, pl.ds(BLOCK, BLOCK)], step1.at[l, 1], s.at[5], r.at[5], down_peer)
        to_up, to_down, here = mine(after), mine(before), mine(y)
        got(step1.at[l, 0], s.at[4], r.at[4])
        step_out[l, 1, :BLOCK, :] = (to_up[:BLOCK] + step1[l, 0].astype(f32)).astype(bf16)
        step_out[l, 1, BLOCK:, :] = to_up[BLOCK:].astype(bf16)
        put(step_out.at[l, 1], step2.at[l, 0], s.at[6], r.at[6], up_peer)
        got(step1.at[l, 1], s.at[5], r.at[5])
        step_out[l, 2, :BLOCK, :] = to_down[:BLOCK].astype(bf16)
        step_out[l, 2, BLOCK:, :] = (to_down[BLOCK:] + step1[l, 1].astype(f32)).astype(bf16)
        put(step_out.at[l, 2], step2.at[l, 1], s.at[7], r.at[7], down_peer)
        got(step2.at[l, 0], s.at[6], r.at[6])
        got(step2.at[l, 1], s.at[7], r.at[7])
        return here + step2[l, 0].astype(f32) + step2[l, 1].astype(f32)

    def attend_back(l, grad_att):
        q3 = by_head(q[l], q_masks).astype(bf16)
        do3 = by_head(grad_att, v_masks)
        o3 = by_head(att[l], v_masks)
        delta = jnp.sum((do3 * o3).T, axis=0, keepdims=True)
        do3 = do3.astype(bf16)
        acc[...] = jnp.zeros_like(acc)
        log_total = lse[l]

        def step(i, carry):
            at = pl.ds(pl.multiple_of(i * PIECE, PIECE), PIECE)
            k = kv[l, at, 0:256]
            s = jnp.where(keep_ref[at, :] < 0, negative, dot_t(k, q3))
            p = jnp.exp(s - log_total)
            ds = (p * (dot_t(kv[l, at, 128:384], do3) - delta)).astype(bf16)
            dk = dot(ds, q3)
            dv = dot(p.astype(bf16), do3)
            dkv[l, at, 0:128] = dk[:, :128].astype(bf16)
            dkv[l, at, 128:256] = (dk[:, 128:] + dv[:, :128]).astype(bf16)
            dkv[l, at, 256:384] = dv[:, 128:].astype(bf16)
            acc[...] += dot(k.T, ds)
            return carry

        lax.fori_loop(0, KEYS // PIECE, step, 0)
        dqkv[l, :, 0:256] = (from_heads(acc[...].T, q_masks) * 0.125).astype(bf16)

    def backward(l, dout_q, gdi_ref, x_q):
        base = 8 + 4 * (1 - l)
        row = small[l]
        gdi = gdi_ref[...]
        gpre = (dot(gdi, w_ref[l, :, DOWN0:WIDE]) * slope[l]).astype(bf16)
        part[4 + 2 * l] = dot_t(gpre, w_ref[l, :, UP0:DOWN0]).astype(bf16)
        sum_start(base, 4 + 2 * l)
        grads_ref[l, :, UP0:DOWN0] = dot(n2[l].T, gpre).astype(bf16)
        grads_ref[l, :, DOWN0:WIDE] = dot(gdi.T, act[l]).astype(bf16)
        little[l] = jnp.zeros_like(little[l])
        little[l, 6:7, :] = jnp.sum(gpre.astype(f32), axis=0, keepdims=True)
        little[l, 5:6, :] = jnp.sum(dout_q, axis=0, keepdims=True)
        c = sum_wait(base, 4 + 2 * l)
        gv, g_gain, g_shift = norm_back(mid[l], row[1:2], c)
        gm = dout_q + gv
        low = gm.astype(bf16)
        ga[l, quarter, :] = low
        share_start(base + 1, ga.at[l])
        little[l, 1:2, :] = g_gain
        little[l, 3:4, :] = g_shift
        little[l, 4:5, :] = jnp.sum(low.astype(f32), axis=0, keepdims=True)
        share_wait(base + 1, ga.at[l])
        grad_att = dot(ga[l], w_ref[l, :, OUT0:UP0]).astype(bf16)
        attend_back(l, grad_att)
        dqkv[l, :, 256:640] = dkv_sum(l).astype(bf16)
        part[5 + 2 * l] = dot_t(dqkv[l], w_ref[l, :, Q0:OUT0]).astype(bf16)
        sum_start(base + 2, 5 + 2 * l)
        grads_ref[l, :, Q0:OUT0] = dot(n1[l].T, dqkv[l]).astype(bf16)
        sums = jnp.sum(dqkv[l].astype(f32), axis=0, keepdims=True)
        wide_col = lax.broadcasted_iota(jnp.int32, (8, 640), 1)
        which = lax.broadcasted_iota(jnp.int32, (8, 640), 0)
        two = jnp.where(((wide_col < 256) & (which == 0)) | ((wide_col >= 256) & (which == 1)), sums, 0.0)
        placed = dot_t(two.astype(bf16), sel_ref[...])
        little[l, 7:9, :] = placed[0:2]
        c = sum_wait(base + 2, 5 + 2 * l)
        gv, g_gain, g_shift = norm_back(x_q, row[0:1], c)
        little[l, 0:1, :] = g_gain
        little[l, 2:3, :] = g_shift
        gx = gm + gv
        kept_ref[l, 1] = gx.astype(bf16)
        return gx

    def out_grads(l):
        both = dot(ga[l].T, att[l])
        grads_ref[l, :, OUT0 : OUT0 + 128] = (both[:, :128] + little[l].T).astype(bf16)
        grads_ref[l, :, OUT0 + 128 : UP0] = both[:, 128:].astype(bf16)

    load_small(0)
    n1[0] = norm(x_ref[...].astype(f32), small[0, 0:1, :], small[0, 2:3, :]).astype(bf16)
    x0 = x_ref[quarter, :].astype(f32)
    x1 = forward(0, x0).astype(bf16).astype(f32)
    load_small(1)
    n1[1, quarter, :] = norm(x1, small[1, 0:1, :], small[1, 2:3, :]).astype(bf16)
    share_start(3, n1.at[1])
    share_wait(3, n1.at[1])
    forward(1, x1)
    gx = backward(1, g_ref[quarter, :].astype(f32), g_ref, x1).astype(bf16)
    gdi0[quarter, :] = gx
    share_start(11, gdi0)
    out_grads(1)
    share_wait(11, gdi0)
    backward(0, gx.astype(f32), gdi0, x0)
    out_grads(0)
    for copy in sent:
        copy.wait_send()


def layers_call(w, x, g, keep, sel):
    vmem = pl.BlockSpec(memory_space=pltpu.VMEM)
    return pl.pallas_call(
        layers_kernel,
        out_shape=(
            jax.ShapeDtypeStruct((2, 2, QUARTER, D), bf16),
            jax.ShapeDtypeStruct((2, D, WIDE), bf16),
        ),
        in_specs=[pl.BlockSpec(memory_space=pl.ANY)] + [vmem] * 4,
        out_specs=(vmem, vmem),
        scratch_shapes=[
            pltpu.VMEM((2, D, WIDE), bf16),
            pltpu.SemaphoreType.DMA((2,)),
            pltpu.VMEM((2, ROWS, D), bf16),
            pltpu.VMEM((2, ROWS, D), bf16),
            pltpu.VMEM((ROWS, D), bf16),
            pltpu.VMEM((2, ROWS, D), bf16),
            pltpu.VMEM((8, 3, QUARTER, D), bf16),
            pltpu.VMEM((8, ROWS, D), bf16),
            pltpu.VMEM((2, KEYS, 384), bf16),
            pltpu.VMEM((2, ROWS, 256), bf16),
            pltpu.VMEM((2, ROWS, D), bf16),
            pltpu.VMEM((2, ROWS, D), f32),
            pltpu.VMEM((2, QUARTER, D), f32),
            pltpu.VMEM((2, 1, 3 * ROWS), f32),
            pltpu.VMEM((2, ROWS, 256), bf16),
            pltpu.VMEM((2, 16, D), f32),
            pltpu.VMEM((KEYS, 3 * ROWS), f32),
            pltpu.VMEM((256, 3 * ROWS), f32),
            pltpu.VMEM((2, KEYS, 384), bf16),
            pltpu.VMEM((2, ROWS, 640), bf16),
            pltpu.VMEM((2, 4, ROWS, 384), bf16),
            pltpu.VMEM((2, 3, ROWS, 384), bf16),
            pltpu.VMEM((2, 2, BLOCK, 384), bf16),
            pltpu.VMEM((2, 2, ROWS, 384), bf16),
            pltpu.VMEM((2, 128, D), f32),
            pltpu.SemaphoreType.DMA((16, 3)),
            pltpu.SemaphoreType.DMA((16, 3)),
            pltpu.SemaphoreType.DMA((4, 9)),
            pltpu.SemaphoreType.DMA((4, 9)),
        ],
        compiler_params=pltpu.CompilerParams(
            collective_id=1, has_side_effects=True, vmem_limit_bytes=VMEM_LIMIT
        ),
        name="layers",
    )(w, x, g, keep, sel)


def scatter_kernel(
    g_ref, kept_ref, own_ref, tile_ref, dist_ref,
    core_in, halves0, halves1, fulls, out1, out2, tiles, send, recv, d_send, d_recv, t_send, t_recv, d_local,
):
    y, z, core, t = where_am_i()
    other = 1 - core
    zh = lax.div(z, 2)
    h = lax.div(t, 2)

    def spot(da, db):
        return ring(y, da * core + db * other), ring(z, da * other + db * core)

    def peer(da, db):
        yy, zz = spot(da, db)
        return ident(yy, zz, core, t)

    def rows_at(yy, zz, of_core):
        return pl.ds(pl.multiple_of((yy * 4 + lax.div(zz, 2) * 2 + of_core) * SHARD, SHARD), SHARD)

    mate = ident(y, z, other, t)
    plane = [ident(y, ring(z, a), core, ring(t, b)) for a in range(4) for b in range(4) if a or b]
    greet(plane + [ident(ring(y, 1), z, core, t), ident(ring(y, 3), z, core, t), mate])
    sent = []

    def put(src, dst, s, r, to):
        copy = remote(src, dst, s, r, to)
        copy.start()
        sent.append(copy)

    def got(region, s, r):
        remote(region, region, s, r, mate).wait_recv()

    for yy in range(4):
        for zz in range(4):
            k = 20 + yy * 4 + zz
            put(g_ref.at[zz % 2, rows_at(yy, zz, other)], core_in.at[yy * 4 + zz], send.at[k], recv.at[k], mate)

    for l in range(2):
        for a in range(4):
            to_z = h * 2 + l
            here = jnp.logical_and(to_z == z, t == a)
            dst = dist_ref.at[z, lax.rem(t, 2)]

            @pl.when(here)
            def _():
                pltpu.make_async_copy(kept_ref.at[l], dst, d_local).start()

            @pl.when(jnp.logical_not(here))
            def _():
                remote(kept_ref.at[l], dst, d_send.at[l, a], d_recv.at[z, lax.rem(t, 2)],
                       ident(y, to_z, core, a)).start()

    def mine(da, db):
        yy, zz = spot(da, db)
        return g_ref[lax.rem(zz, 2), rows_at(yy, zz, core), :].astype(f32) + core_in[yy * 4 + zz].astype(f32)

    for k in range(16):
        got(core_in.at[k], send.at[20 + k], recv.at[20 + k])

    def first(j, far, to):
        out1[j] = far.astype(bf16)
        k = 4 * j
        put(out1.at[j, :, pl.ds(0, HALF)], halves0.at[j], send.at[k], recv.at[k], to[0])
        put(out1.at[j, :, pl.ds(HALF, WIDE - HALF)], halves1.at[j], send.at[k + 1], recv.at[k + 1], to[1])

    def second(j, ahead, behind, to):
        k = 4 * j
        got(halves0.at[j], send.at[k], recv.at[k])
        out2[j, 0, :, :HALF] = (ahead[:, :HALF] + halves0[j].astype(f32)).astype(bf16)
        out2[j, 0, :, HALF:] = ahead[:, HALF:].astype(bf16)
        put(out2.at[j, 0], fulls.at[j, 0], send.at[k + 2], recv.at[k + 2], to[0])
        got(halves1.at[j], send.at[k + 1], recv.at[k + 1])
        out2[j, 1, :, :HALF] = behind[:, :HALF].astype(bf16)
        out2[j, 1, :, HALF:] = (behind[:, HALF:] + halves1[j].astype(f32)).astype(bf16)
        put(out2.at[j, 1], fulls.at[j, 1], send.at[k + 3], recv.at[k + 3], to[1])

    def third(j, own):
        k = 4 * j
        got(fulls.at[j, 0], send.at[k + 2], recv.at[k + 2])
        got(fulls.at[j, 1], send.at[k + 3], recv.at[k + 3])
        return own + fulls[j, 0].astype(f32) + fulls[j, 1].astype(f32)

    ring_b = (peer(0, 1), peer(0, 3))
    ring_a = (peer(1, 0), peer(3, 0))
    order = (2, 1, 3, 0)
    for da in order:
        first(da, mine(da, 2), ring_b)
    for da in order:
        second(da, mine(da, 1), mine(da, 3), ring_b)
    first(4, third(2, mine(2, 0)), ring_a)
    second(4, third(1, mine(1, 0)), third(3, mine(3, 0)), ring_a)
    total = third(4, third(0, mine(0, 0)))
    own_ref[...] = total
    tiles[0] = total[:, OUT0 : OUT0 + 128]
    for d in (1, 2, 3):
        put(tiles.at[0], tiles.at[d], t_send.at[d - 1], t_recv.at[d - 1], ident(y, z, core, ring(t, d)))
    tile = tiles[0]
    for d in (1, 2, 3):
        got(tiles.at[d], t_send.at[d - 1], t_recv.at[d - 1])
        tile = tile + tiles[d]
    tile_ref[...] = tile

    for l in range(2):
        for a in range(4):
            to_z = h * 2 + l
            here = jnp.logical_and(to_z == z, t == a)
            dst = dist_ref.at[z, lax.rem(t, 2)]

            @pl.when(here)
            def _():
                pltpu.make_async_copy(kept_ref.at[l], dst, d_local).wait()

            @pl.when(jnp.logical_not(here))
            def _():
                remote(kept_ref.at[l], dst, d_send.at[l, a], d_recv.at[z, lax.rem(t, 2)],
                       ident(y, to_z, core, a)).wait_send()

    for zz in range(4):
        for b in range(2):
            from_here = jnp.logical_and(zz == z, t == zh * 2 + b)

            @pl.when(jnp.logical_not(from_here))
            def _():
                got(dist_ref.at[zz, b], d_send.at[0, 0], d_recv.at[zz, b])

    for copy in sent:
        copy.wait_send()


def scatter_call(grads, kept):
    vmem = pl.BlockSpec(memory_space=pltpu.VMEM)
    return pl.pallas_call(
        scatter_kernel,
        out_shape=(
            jax.ShapeDtypeStruct((SHARD, WIDE), f32),
            jax.ShapeDtypeStruct((SHARD, 128), f32),
            jax.ShapeDtypeStruct((4, 2, 2, QUARTER, D), bf16),
        ),
        in_specs=[vmem] * 2,
        out_specs=(vmem,) * 3,
        scratch_shapes=[
            pltpu.VMEM((16, SHARD, WIDE), bf16),
            pltpu.VMEM((5, SHARD, HALF), bf16),
            pltpu.VMEM((5, SHARD, WIDE - HALF), bf16),
            pltpu.VMEM((5, 2, SHARD, WIDE), bf16),
            pltpu.VMEM((5, SHARD, WIDE), bf16),
            pltpu.VMEM((5, 2, SHARD, WIDE), bf16),
            pltpu.VMEM((4, SHARD, 128), f32),
            pltpu.SemaphoreType.DMA((36,)),
            pltpu.SemaphoreType.DMA((36,)),
            pltpu.SemaphoreType.DMA((2, 4)),
            pltpu.SemaphoreType.DMA((4, 2)),
            pltpu.SemaphoreType.DMA((3,)),
            pltpu.SemaphoreType.DMA((3,)),
            pltpu.SemaphoreType.DMA,
        ],
        compiler_params=pltpu.CompilerParams(
            collective_id=2, has_side_effects=True, vmem_limit_bytes=VMEM_LIMIT
        ),
        name="gradients_to_owners",
    )(grads, kept)


def selection():
    sel = np.zeros((D, 640), np.float32)
    for c in range(16):
        for i in range(12):
            sel[c * 48 + i, c * 12 + i] = 1.0
            sel[c * 48 + i, 448 + c * 12 + i] = 1.0
    return sel


def key_frames():
    r = np.arange(KEYS)
    j, w = r // ROWS, r % ROWS
    y, core = j // 2, j % 2
    hi = w // BLOCK
    return (((y * 2 + hi) * 2 + core) * BLOCK + w % BLOCK).astype(np.int32)


def on_device(
    frames, w_qkv, w_out, w_up, w_down, ln_gains, shifts, qv_bias, up_bias, lengths, out_grad
):
    _, z, _, _ = where_am_i()
    pad = ((0, 0), (0, SHARD - 12))
    little = jnp.concatenate(
        [ln_gains[0], shifts[0], up_bias, jnp.pad(qv_bias[0], pad), jnp.zeros((55, SHARD), bf16)], axis=0
    )
    packed = jnp.concatenate(
        [
            w_qkv[0, :, 0], jnp.zeros((SHARD, 64), bf16), w_qkv[0, :, 1], w_qkv[0, :, 2],
            little.T, w_out[0].T, w_up[0], w_down[0].T,
        ],
        axis=1,
    )
    w_all, x, g = gather_call(packed, frames[:, 0], out_grad[:, 0])
    length = lax.dynamic_index_in_dim(lengths, z, 0, keepdims=False)[0]
    keep = jnp.where(jnp.asarray(key_frames())[:, None] < length, 0.0, -1.0).astype(f32)
    kept, grads = layers_call(w_all, x, g, keep, jnp.asarray(selection(), bf16))
    own, tile, dist = scatter_call(grads, kept)
    outs = dist.astype(f32)
    tile_t = tile.T
    little_t = own[:, OUT0 : OUT0 + 64].T
    grad_qkv = jnp.stack([own[:, 0:192], own[:, 256:448], own[:, 448:640]], axis=1)
    return (
        outs[:, :, 0].reshape(1, 4, 1, BLOCK, D),
        outs[:, :, 1].reshape(1, 4, 1, BLOCK, D),
        grad_qkv[None],
        own[:, OUT0 + 64 : UP0].T[None],
        own[:, UP0:DOWN0][None],
        own[:, DOWN0:WIDE].T[None],
        tile_t[0:2][None],
        tile_t[2:6][None],
        little_t[7:9, :12][None],
        little_t[6:7],
    )


def solution(mesh):
    in_specs = (
        P(None, None, "ctx", None),
        P("section", "ctx", None, "tp"),
        P("section", "tp", "ctx"),
        P("section", "ctx", "tp"),
        P("section", "tp", "ctx"),
        P("section", None, "ctx"),
        P("section", None, "ctx"),
        P("section", None, ("tp", "ctx")),
        P("section", ("tp", "ctx")),
        P(),
        P(None, None, "ctx", None),
    )
    out_specs = (
        P("section", None, None, "ctx", None),
        P("section", None, None, "ctx", None),
        P("section", "ctx", None, "tp"),
        P("section", "tp", "ctx"),
        P("section", "ctx", "tp"),
        P("section", "tp", "ctx"),
        P("section", None, "ctx"),
        P("section", None, "ctx"),
        P("section", None, ("tp", "ctx")),
        P("section", ("tp", "ctx")),
    )
    return jax.shard_map(
        on_device, mesh=mesh, in_specs=in_specs, out_specs=out_specs, check_vma=False
    )
```

time: 1520 us -> 263 us (0.17); the launches traced: 1500 us -> 261 us
  waiting for transfers between devices: 556 us -> 0 us
  local copies, waits for them, and re-layouts: 352 us -> 18.1 us
  Pallas kernels: 0 us -> 240 us
  other arithmetic: 173 us -> 2.03 us
  matrix products: 161 us -> 0 us
  blocking collectives: 154 us -> 0 us
  starting transfers between devices: 82.6 us -> 0 us
  between operations: 20.1 us -> 0.72 us
    unnamed x19 -> x0, waiting for transfers between devices: 316 us -> none
    pallas_call x0 -> x3, Pallas kernels: none -> 240 us  [the longest x1 150 us: layers_call(): pl.pallas_call(layers_kernel, out_shape=(jax.ShapeDtypeStruct((2, 2, QUAR...]
    all_gather x7 -> x0, waiting for transfers between devices: 180 us -> none  [the longest x6 180 us: sent_together(): lax.all_gather(both, axis, axis=dim, tiled=True)]
    dot_general x100 -> x0, matrix products: 161 us -> none  [the longest x5 19.1 us: backward_layer(): jnp.dot(activated.T, grad_down_in, preferred_element_type=jnp.float32)]
    unnamed x661 -> x8, local copies, waits for them, and re-layouts: 121 us -> 3.42 us
    reduce_sum x92 -> x0, other arithmetic: 95.4 us -> none  [the longest x24 34.6 us: normalize(): return center * lax.rsqrt(spread + epsilon) * norm_gain + norm_shift]
    all_gather x3 -> x0, blocking collectives: 73.5 us -> none  [the longest x1 30.6 us: on_device(): lax.all_gather(w_qkv[0], 'ctx', axis=0, tiled=True)]
    all_to_all x16 -> x0, starting transfers between devices: 66.3 us -> none  [sent_to_all(): return lax.all_to_all(copies, axis, split_axis=0, concat_axis=0, tiled=True)]
  transfers between devices with their start and end apart: 37 -> 0, of which waited for: 26 -> 0; matrix products, arithmetic and copies ran while one was open for 22% -> 0% of each run, Pallas kernels for 0% -> 0%
where the time goes in v1:
time: 263 us; the launch traced here: 261 us
  Pallas kernels  240 us (91%)
  local copies, waits for them, and re-layouts  18.1 us (7%)
    pallas_call x1, Pallas kernels, layers_call(): pl.pallas_call(layers_kernel, out_shape=(jax.ShapeDtypeStruct((2, 2, QUAR...  150 us
    pallas_call x1, Pallas kernels, scatter_call(): pl.pallas_call(scatter_kernel, out_shape=(jax.ShapeDtypeStruct((SHARD, WI...  51.5 us
    pallas_call x1, Pallas kernels, gather_call(): pl.pallas_call(gather_kernel, out_shape=(jax.ShapeDtypeStruct((2, D, WIDE...  38.5 us

profile of v1, /device:TPU:1, one launch (start us, length us, event | category | flops | bytes accessed | tf_op | source)
XLA Modules:
  0.0 260.9 jit_solution(10789289482449366270)
XLA Ops:
  0.6 0.0 copy-start
  0.7 0.6 copy-done
  1.3 0.6 constant_dynamic-slice_fusion
  1.9 0.7 copy.34
  2.6 1.4 compare_select_fusion
  4.0 0.8 copy.35
  4.8 0.8 copy.33
  5.5 0.8 copy.36
  6.3 0.1 concatenate.6
  6.4 0.8 slice_bitcast_fusion.8
  7.2 1.7 concatenate.7.w_ref
  8.9 1.1 select_n.13.keep_ref
  10.1 38.5 %weights_to_all.1 = (bf16[2,768,2432]{2,1,0:T(8,128)(2,1)}, bf16[192,768]{1,0:T(8,128)(2,1)}, bf16[192,768]{1,0:T(8,128)(2,1)}) custom-call(bf16[48,2432]{1,0:T(8,128)(2,1)} %concatenate.7.w_ref, bf16[4,96,768]{2,1,0:T(8,128)(2,1)} %bitcast.54, bf16[4,96,768]{2,1,0:T(8,128)(2,1)} %bitcast.55), custom_call_target="tpu_custom_call" | custom-call | tf_op jit(solution)/shard_map/weights_to_all/pallas_call | solution.py:161
  48.5 150.2 %layers.1 = (bf16[2,2,48,768]{3,2,1,0:T(8,128)(2,1)}, bf16[2,768,2432]{2,1,0:T(8,128)(2,1)}) custom-call(bf16[2,768,2432]{2,1,0:T(8,128)(2,1)} %get-tuple-element.18.w_hbm, bf16[192,768]{1,0:T(8,128)(2,1)} %get-tuple-element.19.x_ref, bf16[192,768]{1,0:T(8,128)(2,1)} %get-tuple-element.20.g_ref, f32[1536,1]{1,0:T(8,128)} %select_n.13.keep_ref, ...), custom_call_target="tpu_custom_call" | custom-call | tf_op jit(solution)/shard_map/layers/pallas_call | solution.py:475
  198.7 51.5 %gradients_to_owners.1 = (f32[48,2432]{1,0:T(8,128)}, f32[48,128]{1,0:T(8,128)}, bf16[4,2,2,48,768]{4,3,2,1,0:T(8,128)(2,1)}) custom-call(bf16[2,768,2432]{2,1,0:T(8,128)(2,1)} %get-tuple-element.21.g_ref, bf16[2,2,48,768]{3,2,1,0:T(8,128)(2,1)} %get-tuple-element.22.kept_ref), custom_call_target="tpu_custom_call" | custom-call | tf_op jit(solution)/shard_map/gradients_to_owners/pallas_call | solution.py:652
  250.2 0.0 copy-start.1
  250.2 1.5 copy.38
  251.6 0.7 slice_bitcast_fusion.7
  252.4 0.1 slice.68
  252.5 0.7 copy.39
  253.1 0.1 slice.69
  253.2 0.6 copy.43
  253.8 0.8 slice_bitcast_fusion.6
  254.6 0.7 copy.42
  255.2 1.7 slice_bitcast_fusion.2
  256.9 1.7 slice_bitcast_fusion
  258.6 0.7 maximum_bitcast_fusion
  259.3 0.0 copy-done.1
  259.3 1.7 fusion
  (3 shorter events, 0.0 us)
Async XLA Ops:
  0.6 0.7 copy-start
  250.2 9.1 %copy-start.1 = (bf16[4,2,2,48,768]{4,3,2,1,0:T(8,128)(2,1)S(1)}, bf16[4,2,2,48,768]{4,3,2,1,0:T(8,128)(2,1)}, u32[]{:S(2)}) copy-start(bf16[4,2,2,48,768]{4,3,2,1,0:T(8,128)(2,1)} %get-tuple-element.23) | copy-start | bytes 3538948

commit v2 on v1

v2 whole, which is shorter than its diff:
```python
import functools

import jax
import jax.numpy as jnp
import numpy as np
from jax import lax
from jax.experimental import pallas as pl
from jax.experimental.pallas import tpu as pltpu
from jax.sharding import PartitionSpec as P

MESH = pl.DeviceIdType.MESH
f32 = jnp.float32
bf16 = jnp.bfloat16
epsilon = 1e-05
negative = -1e30

D = 768
SHARD = 48
QUARTER = 48
BLOCK = 96
ROWS = 192
KEYS = 1536
Q0, KV0, OUT0, UP0, DOWN0, WIDE = 0, 256, 640, 896, 1664, 2432
HALF = 1280
PIECE = 256
HEADS3 = 3
VMEM_LIMIT = 60 * 1024 * 1024


def where_am_i():
    s = lax.axis_index("section")
    c = lax.axis_index("ctx")
    t = lax.axis_index("tp")
    y = lax.div(c, 4)
    zh = lax.rem(lax.div(c, 2), 2)
    core = lax.rem(c, 2)
    return y, zh * 2 + s, core, t


def ident(y, z, core, t):
    return {"section": lax.rem(z, 2), "ctx": y * 4 + lax.div(z, 2) * 2 + core, "tp": t}


def ring(i, d):
    return lax.rem(i + d, 4)


def greet(peers):
    barrier = pltpu.get_barrier_semaphore()
    for peer in peers:
        pl.semaphore_signal(barrier, inc=1, device_id=peer, device_id_type=MESH)
    pl.semaphore_wait(barrier, len(peers))


def remote(src, dst, send, recv, peer):
    return pltpu.make_async_remote_copy(
        src_ref=src, dst_ref=dst, send_sem=send, recv_sem=recv, device_id=peer, device_id_type=MESH
    )


def dot(a, b):
    return lax.dot_general(a, b, (((1,), (0,)), ((), ())), preferred_element_type=f32)


def dot_t(a, b):
    return lax.dot_general(a, b, (((1,), (1,)), ((), ())), preferred_element_type=f32)


def hat(v):
    center = v - jnp.mean(v, axis=-1, keepdims=True)
    r = lax.rsqrt(jnp.mean(center * center, axis=-1, keepdims=True) + epsilon)
    return center * r, r


def norm(v, gain, shift):
    return hat(v)[0] * gain + shift


def norm_back(v, gain, c):
    vhat, r = hat(v)
    cg = c * gain
    grad = r * (
        cg - jnp.mean(cg, axis=-1, keepdims=True) - vhat * jnp.mean(cg * vhat, axis=-1, keepdims=True)
    )
    return grad, jnp.sum(c * vhat, axis=0, keepdims=True), jnp.sum(c, axis=0, keepdims=True)


def layers_kernel(
    pack_ref, f_ref, og_ref, keep_ref, sel_ref,
    own_ref, tile_ref, dist_ref,
    w_ref, grads, x_all, g_all, kept, n1, n2, gdi0, ga, rs, part, kv, att, act, slope, mid, lse, q, small,
    scores, acc, dkv, dqkv, core_in, y_in, little,
    cin_a, cin_b, s_a, s_b, zin_a, zin_b, u_a, u_b, yin_a, yin_b, tiles,
    x_send, x_recv, k_send, k_recv, b_send, b_recv, w_send, w_recv, r_send, r_recv, f_send, f_recv,
    d_send, d_recv, d_local, t_send, t_recv,
):
    y, z, core, t = where_am_i()
    other = 1 - core
    zh = lax.div(z, 2)
    mate = ident(y, z, other, t)

    def along_x(d):
        return ident(y, z, core, ring(t, d))

    def along_y(d):
        return ident(ring(y, d), z, core, t)

    def along_z(d):
        return ident(y, ring(z, d), core, t)

    greet(
        [ident(y, ring(z, a), core, ring(t, b)) for a in range(4) for b in range(4) if a or b]
        + [along_y(d) for d in (1, 2, 3)]
        + [mate]
    )
    later = []

    def put(src, dst, send, recv, to, when=None):
        def make():
            return remote(src, dst, send, recv, to)

        if when is None:
            make().start()
        else:
            pl.when(when)(lambda: make().start())
        later.append((when, make))

    def got(region, send, recv):
        remote(region, region, send, recv, mate).wait_recv()


    def cols(half):
        return pl.ds(0, UP0) if half == 0 else pl.ds(UP0, WIDE - UP0)

    first_core, second_core = core == 0, core == 1

    def holds(l):
        return lax.rem(z, 2) == l

    def lacks(l):
        return lax.rem(z, 2) != l

    def w_sems(l, half, i):
        return w_send.at[2 * l + half, i], w_recv.at[2 * l + half, i]

    def gather_a(l, half):
        here = w_ref.at[l, y, zh, core, :, cols(half)]
        src = pack_ref.at[:, cols(half)]
        for d in (1, 3, 2):
            put(src, here, *w_sems(l, half, d - 1), along_z(d), when=first_core & holds(l))
            put(src, here, *w_sems(l, half, d - 1), along_y(d), when=second_core & holds(l))

        @pl.when(holds(l))
        def _():
            w_ref[l, y, zh, core, :, cols(half)] = pack_ref[:, cols(half)]

    def from_z(d):
        return lax.div(ring(z, 4 - d), 2)

    def gather_b(l, half):
        c = cols(half)

        @pl.when(first_core & holds(l))
        def _():
            got(w_ref.at[l, y, from_z(2), core, :, c], *w_sems(l, half, 1))

        @pl.when(first_core & lacks(l))
        def _():
            for d in (1, 3):
                got(w_ref.at[l, y, from_z(d), core, :, c], *w_sems(l, half, d - 1))

        @pl.when(second_core & holds(l))
        def _():
            for d in (1, 3, 2):
                got(w_ref.at[l, ring(y, 4 - d), zh, core, :, c], *w_sems(l, half, d - 1))

        pair = w_ref.at[l, y, :, core, :, c]
        four = w_ref.at[l, :, zh, core, :, c]
        for d in (1, 3, 2):
            put(pair, pair, *w_sems(l, half, 2 + d), along_y(d), when=first_core)
            put(four, four, *w_sems(l, half, 2 + d), along_z(d), when=second_core & holds(l))

    def gather_c(l, half):
        c = cols(half)

        @pl.when(first_core)
        def _():
            for d in (1, 3, 2):
                got(w_ref.at[l, ring(y, 4 - d), :, core, :, c], *w_sems(l, half, 2 + d))

        @pl.when(second_core & holds(l))
        def _():
            got(w_ref.at[l, :, from_z(2), core, :, c], *w_sems(l, half, 4))

        @pl.when(second_core & lacks(l))
        def _():
            for d in (1, 3):
                got(w_ref.at[l, :, from_z(d), core, :, c], *w_sems(l, half, 2 + d))

        mine = w_ref.at[l, :, :, core, :, c]
        put(mine, mine, *w_sems(l, half, 6), mate)

    def gather_d(l, half):
        got(w_ref.at[l, :, :, other, :, cols(half)], *w_sems(l, half, 6))

    def weight(l, first, last):
        return w_ref[l, :, :, :, :, first:last].reshape(D, last - first)


    cin, s_out, zin, u_out, yin = (cin_b, cin_a), (s_b, s_a), (zin_b, zin_a), (u_b, u_a), (yin_b, yin_a)

    def r_sems(l, half, i):
        return r_send.at[2 * l + half, i], r_recv.at[2 * l + half, i]

    def keep_grad(l, first, value):
        n = value.shape[1]
        grads[l, :, :, :, :, first : first + n] = value.astype(bf16).reshape(4, 2, 2, SHARD, n)

    def scatter_a(l, half):
        put(grads.at[l, :, :, other, :, cols(half)], cin[half].at[l], *r_sems(l, half, 0), mate)

    def scatter_b(l, half):
        got(cin[half].at[l], *r_sems(l, half, 0))

        def add(i, carry):
            for b in range(2):
                s_out[half][l, i, b] = (
                    grads[l, i, b, core, :, cols(half)].astype(f32) + cin[half][l, i, b].astype(f32)
                ).astype(bf16)
            return carry

        lax.fori_loop(0, 4, add, 0)
        for d in (1, 3, 2):
            put(s_out[half].at[l, :, lax.div(ring(z, d), 2)], zin[half].at[d - 1], *r_sems(l, half, d),
                along_z(d), when=holds(l) if d == 2 else lacks(l))

    def scatter_c(l, half):
        @pl.when(holds(l))
        def _():
            for d in (1, 3, 2):
                got(zin[half].at[d - 1], *r_sems(l, half, d))

            def add(i, carry):
                total = s_out[half][l, i, zh].astype(f32)
                for d in (1, 2, 3):
                    total = total + zin[half][d - 1, i].astype(f32)
                u_out[half][i] = total.astype(bf16)
                return carry

            lax.fori_loop(0, 4, add, 0)

        for d in (2, 1, 3):
            put(u_out[half].at[ring(y, d)], yin[half].at[d - 1], *r_sems(l, half, 3 + d), along_y(d),
                when=holds(l))

    def scatter_d(l, half):
        @pl.when(holds(l))
        def _():
            total = u_out[half][y].astype(f32)
            for d in (1, 3, 2):
                got(yin[half].at[d - 1], *r_sems(l, half, 3 + d))
                total = total + yin[half][d - 1].astype(f32)
            own_ref[:, cols(half)] = total


    h = lax.div(t, 2)

    def place(l, kind):
        to_z = h * 2 + l
        dst = dist_ref.at[z, lax.rem(t, 2), kind]
        for a in range(4):
            here = jnp.logical_and(to_z == z, t == a)
            put(kept.at[l, kind], dst, d_send.at[2 * l + kind, a], d_recv.at[z, lax.rem(t, 2), kind],
                ident(y, to_z, core, a), when=jnp.logical_not(here))

        def make():
            return pltpu.make_async_copy(kept.at[l, kind], dst, d_local.at[kind])

        pl.when(to_z == z)(lambda: make().start())
        placed.append((to_z == z, make))

    placed = []


    quarter = pl.ds(pl.multiple_of(t * QUARTER, QUARTER), QUARTER)

    def rows_of(i):
        return pl.ds(pl.multiple_of(i * QUARTER, QUARTER), QUARTER)

    def share_start(phase, ref):
        for d in (1, 3, 2):
            put(ref.at[quarter], ref.at[quarter], x_send.at[phase, d - 1], x_recv.at[phase, d - 1], along_x(d))

    def share_wait(phase, ref):
        for d in (1, 3, 2):
            got(ref.at[rows_of(ring(t, 4 - d))], x_send.at[phase, d - 1], x_recv.at[phase, d - 1])

    def sum_start(phase, i):
        for d in (1, 3, 2):
            put(part.at[i, rows_of(ring(t, d))], rs.at[i, d - 1], x_send.at[phase, d - 1],
                x_recv.at[phase, d - 1], along_x(d))

    def sum_wait(phase, i):
        total = part[i, quarter, :].astype(f32)
        for d in (1, 3, 2):
            got(rs.at[i, d - 1], x_send.at[phase, d - 1], x_recv.at[phase, d - 1])
            total = total + rs[i, d - 1].astype(f32)
        return total


    col = lax.broadcasted_iota(jnp.int32, (1, 256), 1)
    q_masks = [jnp.where((col >= 64 * i) & (col < 64 * i + 64), 1.0, 0.0).astype(f32) for i in range(3)]
    v_masks = [jnp.where((col >= 64 * i + 64) & (col < 64 * i + 128), 1.0, 0.0).astype(f32) for i in range(3)]

    def by_head(rows, masks):
        rows = rows.astype(f32)
        return jnp.concatenate([rows * m for m in masks], axis=0)

    def from_heads(rows, masks):
        return sum(rows[i * ROWS : (i + 1) * ROWS] * masks[i] for i in range(3))

    def key_rows(b):
        return pl.ds(pl.multiple_of(b * ROWS, ROWS), ROWS)

    def attend(l, meanwhile):
        def sems(i):
            return k_send.at[l, i], k_recv.at[l, i]

        own = y * 2 + core
        for d in (1, 3, 2):
            put(kv.at[l, own], kv.at[l, own], *sems(d - 1), along_y(d))
        put(kv.at[l, own], kv.at[l, own], *sems(3), mate)
        meanwhile()
        q3 = by_head(q[l], q_masks).astype(bf16)

        def first(b, top):
            s = dot_t(kv[l, b, :, 0:256], q3)
            s = jnp.where(keep_ref[key_rows(b), :] < 0, negative, s)
            scores[key_rows(b), :] = s
            return jnp.maximum(top, jnp.max(s, axis=0, keepdims=True))

        top = first(own, jnp.full((1, 3 * ROWS), negative, f32))
        got(kv.at[l, y * 2 + other], *sems(3))
        top = first(y * 2 + other, top)

        def same_core(i, top):
            d = 1 + 2 * i - 3 * lax.div(i, 2)
            b = ring(y, 4 - d) * 2 + core
            got(kv.at[l, b], *sems(d - 1))
            remote(kv.at[l, b], kv.at[l, b], *sems(3 + d), mate).start()
            return first(b, top)

        top = lax.fori_loop(0, 3, same_core, top)
        for d in (1, 2, 3):
            b = ring(y, 4 - d) * 2 + core
            later.append((None, functools.partial(remote, kv.at[l, b], kv.at[l, b], *sems(3 + d), mate)))

        def other_core(i, top):
            d = 1 + 2 * i - 3 * lax.div(i, 2)
            b = ring(y, 4 - d) * 2 + other
            got(kv.at[l, b], *sems(3 + d))
            return first(b, top)

        top = lax.fori_loop(0, 3, other_core, top)
        acc[...] = jnp.zeros_like(acc)

        def second(b, total):
            p = jnp.exp(scores[key_rows(b), :] - top)
            acc[...] += dot(kv[l, b, :, 128:384].T, p.astype(bf16))
            return total + jnp.sum(p, axis=0, keepdims=True)

        total = lax.fori_loop(0, 8, second, jnp.zeros((1, 3 * ROWS), f32))
        lse[l] = top + jnp.log(total)
        att[l] = from_heads((acc[...] / total).T, v_masks).astype(bf16)

    def attend_back(l, grad_att, meanwhile):
        def sems(i):
            return b_send.at[l, i], b_recv.at[l, i]

        q3 = by_head(q[l], q_masks).astype(bf16)
        do3 = by_head(grad_att, v_masks)
        delta = jnp.sum((do3 * by_head(att[l], v_masks)).T, axis=0, keepdims=True)
        do3 = do3.astype(bf16)
        acc[...] = jnp.zeros_like(acc)
        log_total = lse[l]

        def block(b):
            k = kv[l, b, :, 0:256]
            s = jnp.where(keep_ref[key_rows(b), :] < 0, negative, dot_t(k, q3))
            p = jnp.exp(s - log_total)
            ds = (p * (dot_t(kv[l, b, :, 128:384], do3) - delta)).astype(bf16)
            dk = dot(ds, q3)
            dv = dot(p.astype(bf16), do3)
            acc[...] += dot(k.T, ds)
            return jnp.concatenate([dk[:, :128], dk[:, 128:] + dv[:, :128], dv[:, 128:]], axis=1)

        def for_mate(i, carry):
            off = 3 - i
            b = ring(y, off) * 2 + other
            dkv[l, b] = block(b).astype(bf16)
            remote(dkv.at[l, b], core_in.at[l, off], *sems(off), mate).start()
            return carry

        def for_y(i, carry):
            off = 3 - i
            b = ring(y, off) * 2 + core
            value = block(b)
            got(core_in.at[l, off], *sems(off))
            dkv[l, b] = (value + core_in[l, off].astype(f32)).astype(bf16)
            remote(dkv.at[l, b], y_in.at[l, off - 1], *sems(3 + off), along_y(off)).start()
            return carry

        lax.fori_loop(0, 4, for_mate, 0)
        lax.fori_loop(0, 3, for_y, 0)
        for off in range(4):
            b = ring(y, off) * 2 + other
            later.append((None, functools.partial(remote, dkv.at[l, b], core_in.at[l, off], *sems(off), mate)))
        for off in (1, 2, 3):
            b = ring(y, off) * 2 + core
            later.append((None, functools.partial(
                remote, dkv.at[l, b], y_in.at[l, off - 1], *sems(3 + off), along_y(off))))
        total = block(y * 2 + core)
        dqkv[l, :, 0:256] = (from_heads(acc[...].T, q_masks) * 0.125).astype(bf16)
        got(core_in.at[l, 0], *sems(0))
        total = total + core_in[l, 0].astype(f32)
        meanwhile()
        for off in (1, 3, 2):
            got(y_in.at[l, off - 1], *sems(3 + off))
            total = total + y_in[l, off - 1].astype(f32)
        dqkv[l, :, 256:640] = total.astype(bf16)


    def load_small(l):
        small[l] = weight(l, OUT0, OUT0 + 128).astype(f32).T[:16]

    def forward(l, x_q, on_kv, on_sum, on_share, on_last):
        row = small[l]
        bias = dot(row.astype(bf16), sel_ref[...])
        wide = dot(n1[l], weight(l, Q0, OUT0))
        kv[l, y * 2 + core] = (wide[:, 256:] + bias[8:9, 256:]).astype(bf16)
        q[l] = ((wide[:, :256] + bias[7:8, :256]).astype(bf16).astype(f32) * 0.125).astype(bf16)
        attend(l, on_kv)
        part[2 * l] = dot_t(att[l], weight(l, OUT0, UP0)).astype(bf16)
        sum_start(4 * l, 2 * l)
        on_sum()
        m = x_q + sum_wait(4 * l, 2 * l) + row[4:5]
        mid[l] = m
        n2[l, quarter, :] = norm(m, row[1:2], row[3:4]).astype(bf16)
        share_start(4 * l + 1, n2.at[l])
        on_share()
        share_wait(4 * l + 1, n2.at[l])
        u = dot(n2[l], weight(l, UP0, DOWN0)) + row[6:7]
        phi = 0.5 * (1.0 + lax.erf(u * np.float32(0.5**0.5)))
        act[l] = (u * phi).astype(bf16)
        part[2 * l + 1] = dot_t(act[l], weight(l, DOWN0, WIDE)).astype(bf16)
        sum_start(4 * l + 2, 2 * l + 1)
        slope[l] = phi + u * jnp.exp(-0.5 * u * u) * np.float32((2 * np.pi) ** -0.5)
        on_last()
        out = m + sum_wait(4 * l + 2, 2 * l + 1) + row[5:6]
        kept[l, 0] = out.astype(bf16)
        return out

    def backward(l, dout_q, gdi_ref, x_q, on_sum, on_share, on_att, on_last):
        base = 8 + 4 * (1 - l)
        row = small[l]
        gdi = gdi_ref[...]
        gpre = (dot(gdi, weight(l, DOWN0, WIDE)) * slope[l]).astype(bf16)
        part[4 + 2 * l] = dot_t(gpre, weight(l, UP0, DOWN0)).astype(bf16)
        sum_start(base, 4 + 2 * l)
        keep_grad(l, UP0, dot(n2[l].T, gpre))
        keep_grad(l, DOWN0, dot(gdi.T, act[l]))
        little[l] = jnp.zeros_like(little[l])
        little[l, 6:7, :] = jnp.sum(gpre.astype(f32), axis=0, keepdims=True)
        little[l, 5:6, :] = jnp.sum(dout_q, axis=0, keepdims=True)
        on_sum()
        c = sum_wait(base, 4 + 2 * l)
        gv, g_gain, g_shift = norm_back(mid[l], row[1:2], c)
        gm = dout_q + gv
        low = gm.astype(bf16)
        ga[l, quarter, :] = low
        share_start(base + 1, ga.at[l])
        little[l, 1:2, :] = g_gain
        little[l, 3:4, :] = g_shift
        little[l, 4:5, :] = jnp.sum(low.astype(f32), axis=0, keepdims=True)
        on_share()
        share_wait(base + 1, ga.at[l])
        attend_back(l, dot(ga[l], weight(l, OUT0, UP0)).astype(bf16), on_att)
        part[5 + 2 * l] = dot_t(dqkv[l], weight(l, Q0, OUT0)).astype(bf16)
        sum_start(base + 2, 5 + 2 * l)
        keep_grad(l, Q0, dot(n1[l].T, dqkv[l]))
        sums = jnp.sum(dqkv[l].astype(f32), axis=0, keepdims=True)
        wide_col = lax.broadcasted_iota(jnp.int32, (8, 640), 1)
        which = lax.broadcasted_iota(jnp.int32, (8, 640), 0)
        two = jnp.where(((wide_col < 256) & (which == 0)) | ((wide_col >= 256) & (which == 1)), sums, 0.0)
        placed_rows = dot_t(two.astype(bf16), sel_ref[...])
        little[l, 7:9, :] = placed_rows[0:2]
        on_last()
        c = sum_wait(base + 2, 5 + 2 * l)
        gv, g_gain, g_shift = norm_back(x_q, row[0:1], c)
        little[l, 0:1, :] = g_gain
        little[l, 2:3, :] = g_shift
        gx = gm + gv
        kept[l, 1] = gx.astype(bf16)
        return gx

    def out_grads(l):
        both = dot(ga[l].T, att[l])
        keep_grad(l, OUT0, jnp.concatenate([both[:, :128] + little[l].T, both[:, 128:]], axis=1))


    A, B = 1, 0
    gather_a(0, B)
    twin = ident(y, 3 - z, core, t)
    mine = pl.ds(pl.multiple_of(zh * BLOCK, BLOCK), BLOCK)
    theirs = pl.ds(pl.multiple_of((1 - zh) * BLOCK, BLOCK), BLOCK)
    put(f_ref.at[3 - z], x_all.at[mine], f_send.at[0], f_recv.at[0], twin)
    gather_a(0, A)
    put(og_ref.at[3 - z], g_all.at[mine], f_send.at[1], f_recv.at[1], twin)
    x_all[mine, :] = f_ref[z]
    g_all[mine, :] = og_ref[z]
    gather_b(0, B)
    gather_c(0, B)
    gather_b(0, A)
    got(x_all.at[theirs], f_send.at[0], f_recv.at[0])
    gather_d(0, B)
    load_small(0)
    n1[0] = norm(x_all[...].astype(f32), small[0, 0:1, :], small[0, 2:3, :]).astype(bf16)
    x0 = x_all[quarter, :].astype(f32)

    def run(*steps):
        def body():
            for step in steps:
                step[0](*step[1:])

        return body

    x1 = forward(
        0, x0,
        run((gather_c, 0, A), (gather_a, 1, B), (gather_a, 1, A)),
        run((gather_d, 0, A), (gather_b, 1, B)),
        run((gather_b, 1, A)),
        run((gather_c, 1, B), (gather_c, 1, A)),
    ).astype(bf16).astype(f32)
    gather_d(1, B)
    load_small(1)
    n1[1, quarter, :] = norm(x1, small[1, 0:1, :], small[1, 2:3, :]).astype(bf16)
    share_start(3, n1.at[1])
    share_wait(3, n1.at[1])
    forward(1, x1, run((place, 0, 0)), run((gather_d, 1, A)), run(), run())
    got(g_all.at[theirs], f_send.at[1], f_recv.at[1])
    gx = backward(
        1, g_all[quarter, :].astype(f32), g_all, x1,
        run((scatter_a, 1, A)), run((scatter_b, 1, A)), run((place, 1, 0)), run((scatter_c, 1, A)),
    ).astype(bf16)
    gdi0[quarter, :] = gx
    share_start(11, gdi0)
    out_grads(1)
    scatter_a(1, B)
    share_wait(11, gdi0)
    backward(
        0, gx.astype(f32), gdi0, x0,
        run((scatter_a, 0, A), (scatter_b, 1, B)), run((scatter_b, 0, A)), run((place, 1, 1)),
        run((scatter_c, 0, A), (scatter_c, 1, B)),
    )
    out_grads(0)
    scatter_a(0, B)
    place(0, 1)
    scatter_d(1, A)
    scatter_d(0, A)
    scatter_b(0, B)
    scatter_d(1, B)
    scatter_c(0, B)
    scatter_d(0, B)
    tiles[0] = own_ref[:, OUT0 : OUT0 + 128]
    for d in (1, 2, 3):
        put(tiles.at[0], tiles.at[d], t_send.at[d - 1], t_recv.at[d - 1], along_x(d))
    tile = tiles[0]
    for d in (1, 2, 3):
        got(tiles.at[d], t_send.at[d - 1], t_recv.at[d - 1])
        tile = tile + tiles[d]
    tile_ref[...] = tile
    for kind in range(2):
        for zz in range(4):
            for b in range(2):
                away = jnp.logical_not(jnp.logical_and(zz == z, t == zh * 2 + b))

                @pl.when(away)
                def _():
                    got(dist_ref.at[zz, b, kind], d_send.at[0, 0], d_recv.at[zz, b, kind])

    for when, make in placed:
        pl.when(when)(lambda: make().wait())
    for when, make in later:
        if when is None:
            make().wait_send()
        else:
            pl.when(when)(lambda: make().wait_send())


def layers_call(packed, frames, out_grad, keep, sel):
    vmem = pl.BlockSpec(memory_space=pltpu.VMEM)
    wide_a, wide_b = WIDE - UP0, UP0
    dma = pltpu.SemaphoreType.DMA
    return pl.pallas_call(
        layers_kernel,
        out_shape=(
            jax.ShapeDtypeStruct((SHARD, WIDE), f32),
            jax.ShapeDtypeStruct((SHARD, 128), f32),
            jax.ShapeDtypeStruct((4, 2, 2, QUARTER, D), bf16),
        ),
        in_specs=[vmem] * 5,
        out_specs=(vmem, vmem, pl.BlockSpec(memory_space=pl.ANY)),
        scratch_shapes=[
            pltpu.VMEM((2, 4, 2, 2, SHARD, WIDE), bf16),
            pltpu.VMEM((2, 4, 2, 2, SHARD, WIDE), bf16),
            pltpu.VMEM((ROWS, D), bf16),
            pltpu.VMEM((ROWS, D), bf16),
            pltpu.VMEM((2, 2, QUARTER, D), bf16),
            pltpu.VMEM((2, ROWS, D), bf16),
            pltpu.VMEM((2, ROWS, D), bf16),
            pltpu.VMEM((ROWS, D), bf16),
            pltpu.VMEM((2, ROWS, D), bf16),
            pltpu.VMEM((8, 3, QUARTER, D), bf16),
            pltpu.VMEM((8, ROWS, D), bf16),
            pltpu.VMEM((2, 8, ROWS, 384), bf16),
            pltpu.VMEM((2, ROWS, 256), bf16),
            pltpu.VMEM((2, ROWS, D), bf16),
            pltpu.VMEM((2, ROWS, D), f32),
            pltpu.VMEM((2, QUARTER, D), f32),
            pltpu.VMEM((2, 1, 3 * ROWS), f32),
            pltpu.VMEM((2, ROWS, 256), bf16),
            pltpu.VMEM((2, 16, D), f32),
            pltpu.VMEM((KEYS, 3 * ROWS), f32),
            pltpu.VMEM((256, 3 * ROWS), f32),
            pltpu.VMEM((2, 8, ROWS, 384), bf16),
            pltpu.VMEM((2, ROWS, 640), bf16),
            pltpu.VMEM((2, 4, ROWS, 384), bf16),
            pltpu.VMEM((2, 3, ROWS, 384), bf16),
            pltpu.VMEM((2, 128, D), f32),
            pltpu.VMEM((2, 4, 2, SHARD, wide_a), bf16),
            pltpu.VMEM((2, 4, 2, SHARD, wide_b), bf16),
            pltpu.VMEM((2, 4, 2, SHARD, wide_a), bf16),
            pltpu.VMEM((2, 4, 2, SHARD, wide_b), bf16),
            pltpu.VMEM((3, 4, SHARD, wide_a), bf16),
            pltpu.VMEM((3, 4, SHARD, wide_b), bf16),
            pltpu.VMEM((4, SHARD, wide_a), bf16),
            pltpu.VMEM((4, SHARD, wide_b), bf16),
            pltpu.VMEM((3, SHARD, wide_a), bf16),
            pltpu.VMEM((3, SHARD, wide_b), bf16),
            pltpu.VMEM((4, SHARD, 128), f32),
            dma((16, 3)), dma((16, 3)),
            dma((2, 7)), dma((2, 7)),
            dma((2, 7)), dma((2, 7)),
            dma((4, 7)), dma((4, 7)),
            dma((4, 7)), dma((4, 7)),
            dma((2,)), dma((2,)),
            dma((4, 4)), dma((4, 2, 2)), dma((2,)),
            dma((3,)), dma((3,)),
        ],
        compiler_params=pltpu.CompilerParams(
            collective_id=0, has_side_effects=True, vmem_limit_bytes=VMEM_LIMIT
        ),
        name="layers",
    )(packed, frames, out_grad, keep, sel)


def selection():
    sel = np.zeros((D, 640), np.float32)
    for c in range(16):
        for i in range(12):
            sel[c * 48 + i, c * 12 + i] = 1.0
            sel[c * 48 + i, 448 + c * 12 + i] = 1.0
    return sel


def key_frames():
    r = np.arange(KEYS)
    j, w = r // ROWS, r % ROWS
    y, core = j // 2, j % 2
    hi = w // BLOCK
    return (((y * 2 + hi) * 2 + core) * BLOCK + w % BLOCK).astype(np.int32)


def on_device(
    frames, w_qkv, w_out, w_up, w_down, ln_gains, shifts, qv_bias, up_bias, lengths, out_grad
):
    _, z, _, _ = where_am_i()
    pad = ((0, 0), (0, SHARD - 12))
    little = jnp.concatenate(
        [ln_gains[0], shifts[0], up_bias, jnp.pad(qv_bias[0], pad), jnp.zeros((55, SHARD), bf16)], axis=0
    )
    packed = jnp.concatenate(
        [
            w_qkv[0, :, 0], jnp.zeros((SHARD, 64), bf16), w_qkv[0, :, 1], w_qkv[0, :, 2],
            little.T, w_out[0].T, w_up[0], w_down[0].T,
        ],
        axis=1,
    )
    length = lax.dynamic_index_in_dim(lengths, z, 0, keepdims=False)[0]
    keep = jnp.where(jnp.asarray(key_frames())[:, None] < length, 0.0, -1.0).astype(f32)
    own, tile, dist = layers_call(
        packed, frames[:, 0], out_grad[:, 0], keep, jnp.asarray(selection(), bf16)
    )
    outs = dist.astype(f32)
    tile_t = tile.T
    little_t = own[:, OUT0 : OUT0 + 64].T
    grad_qkv = jnp.stack([own[:, 0:192], own[:, 256:448], own[:, 448:640]], axis=1)
    return (
        outs[:, :, 0].reshape(1, 4, 1, BLOCK, D),
        outs[:, :, 1].reshape(1, 4, 1, BLOCK, D),
        grad_qkv[None],
        own[:, OUT0 + 64 : UP0].T[None],
        own[:, UP0:DOWN0][None],
        own[:, DOWN0:WIDE].T[None],
        tile_t[0:2][None],
        tile_t[2:6][None],
        little_t[7:9, :12][None],
        little_t[6:7],
    )


def solution(mesh):
    in_specs = (
        P(None, None, "ctx", None),
        P("section", "ctx", None, "tp"),
        P("section", "tp", "ctx"),
        P("section", "ctx", "tp"),
        P("section", "tp", "ctx"),
        P("section", None, "ctx"),
        P("section", None, "ctx"),
        P("section", None, ("tp", "ctx")),
        P("section", ("tp", "ctx")),
        P(),
        P(None, None, "ctx", None),
    )
    out_specs = (
        P("section", None, None, "ctx", None),
        P("section", None, None, "ctx", None),
        P("section", "ctx", None, "tp"),
        P("section", "tp", "ctx"),
        P("section", "ctx", "tp"),
        P("section", "tp", "ctx"),
        P("section", None, "ctx"),
        P("section", None, "ctx"),
        P("section", None, ("tp", "ctx")),
        P("section", ("tp", "ctx")),
    )
    return jax.shard_map(
        on_device, mesh=mesh, in_specs=in_specs, out_specs=out_specs, check_vma=False
    )
```

time: 263 us -> 225 us (0.86)
  Pallas kernels: 240 us -> 207 us
  local copies, waits for them, and re-layouts: 18.1 us -> 14.5 us
    pallas_call x3 -> x1, Pallas kernels: 240 us -> 207 us  [layers_call(): pl.pallas_call(layers_kernel, out_shape=(jax.ShapeDtypeStruct((SHARD, WID...]
where the time goes in v2:
time: 225 us; the launch traced here: 224 us
  Pallas kernels  207 us (92%)
  local copies, waits for them, and re-layouts  14.5 us (6%)
    pallas_call x1, Pallas kernels, layers_call(): pl.pallas_call(layers_kernel, out_shape=(jax.ShapeDtypeStruct((SHARD, WID...  207 us

profile of v2, /device:TPU:1, one launch (start us, length us, event | category | flops | bytes accessed | tf_op | source)
XLA Modules:
  0.0 223.8 jit_solution(3777401011890269163)
XLA Ops:
  0.6 0.0 copy-start
  0.7 0.8 slice_bitcast_fusion.8
  1.4 0.8 copy.35
  2.2 0.8 copy.33
  3.0 0.8 copy.36
  3.7 0.7 copy.34
  4.5 0.1 concatenate.6
  4.6 1.7 concatenate.7.pack_ref
  6.4 0.0 copy-done
  6.4 0.6 constant_dynamic-slice_fusion
  6.9 1.3 compare_select_fusion
  8.3 1.1 select_n.13.keep_ref
  9.4 206.6 %layers.1 = (f32[48,2432]{1,0:T(8,128)}, f32[48,128]{1,0:T(8,128)}, bf16[4,2,2,48,768]{4,3,2,1,0:T(8,128)(2,1)}) custom-call(bf16[48,2432]{1,0:T(8,128)(2,1)} %concatenate.7.pack_ref, bf16[4,96,768]{2,1,0:T(8,128)(2,1)} %bitcast.54, bf16[4,96,768]{2,1,0:T(8,128)(2,1)} %bitcast.55, f32[1536,1]{1,0:T(8,128)} %select_n.13.keep_ref, ...), custom_call_target="tpu_custom_call" | custom-call | tf_op jit(solution)/shard_map/layers/pallas_call | solution.py:604
  216.0 0.0 copy-start.1
  216.0 2.9 %fusion = (f32[4,2,1,48,768]{4,3,2,1,0:T(8,128)}, f32[4,2,1,48,768]{4,3,2,1,0:T(8,128)}) fusion(bf16[4,2,2,48,768]{4,3,2,1,0:T(8,128)(2,1)} %get-tuple-element.13), kind=kLoop, calls=%fused_computation.14 | loop fusion | bytes 4718592 | tf_op jit(solution)/shard_map/slice | solution.py:710
  219.0 0.0 copy-start.2
  219.0 0.0 copy-done.1
  219.0 0.7 slice_bitcast_fusion.2
  219.7 0.7 maximum_bitcast_fusion
  220.3 0.7 slice_bitcast_fusion
  221.1 0.0 copy-done.2
  221.1 0.6 copy.38
  221.7 0.1 slice_bitcast_fusion.6
  221.8 0.7 copy.42
  222.4 0.1 slice.68
  222.5 0.7 copy.39
  223.2 0.1 slice.69
  223.2 0.6 copy.43
  (4 shorter events, 0.0 us)
Async XLA Ops:
  0.6 5.7 %copy-start = (s32[4,1]{0,1:T(1,128)S(1)}, s32[4,1]{0,1:T(1,128)}, u32[]{:S(2)}) copy-start(s32[4,1]{0,1:T(1,128)} %param.22) | copy-start | bytes 52
  216.0 3.0 %copy-start.1 = (f32[48,2432]{1,0:T(8,128)S(1)}, f32[48,2432]{1,0:T(8,128)}, u32[]{:S(2)}) copy-start(f32[48,2432]{1,0:T(8,128)} %get-tuple-element.14) | copy-start | bytes 1400836
  219.0 2.1 copy-start.2

commit v3 on v2

--- a/solution.py
+++ b/solution.py
@@ -86,9 +86,9 @@
 
 
 def layers_kernel(
-    pack_ref, f_ref, og_ref, keep_ref, sel_ref,
+    f_ref, wqkv_ref, wout_ref, wup_ref, wdown_ref, gains_ref, shifts_ref, qv_ref, up_ref, len_ref, og_ref,
     own_ref, tile_ref, dist_ref,
-    w_ref, grads, x_all, g_all, kept, n1, n2, gdi0, ga, rs, part, kv, att, act, slope, mid, lse, q, small,
+    pack_ref, turned, sel_ref, w_ref, grads, x_all, g_all, x1_all, o1_all, gx1_all, gx0_all, both, n1, n2, ga, rs, part, kv, att, act, slope, mid, lse, q, small,
     scores, acc, dkv, dqkv, core_in, y_in, little,
     cin_a, cin_b, s_a, s_b, zin_a, zin_b, u_a, u_b, yin_a, yin_b, tiles,
     x_send, x_recv, k_send, k_recv, b_send, b_recv, w_send, w_recv, r_send, r_recv, f_send, f_recv,
@@ -109,11 +109,26 @@
         return ident(y, ring(z, d), core, t)
 
     greet(
-        [ident(y, ring(z, a), core, ring(t, b)) for a in range(4) for b in range(4) if a or b]
+        [along_x(d) for d in (1, 2, 3)]
         + [along_y(d) for d in (1, 2, 3)]
+        + [along_z(d) for d in (1, 2, 3)]
         + [mate]
     )
     later = []
+
+
+    turned[...] = jnp.zeros_like(turned)
+    turned[0:2, 0:SHARD] = gains_ref[0].astype(f32)
+    turned[2:6, 0:SHARD] = shifts_ref[0].astype(f32)
+    turned[6:7, 0:SHARD] = up_ref[...].astype(f32)
+    turned[7:9, 0:12] = qv_ref[0].astype(f32)
+    pack_ref[:, OUT0:UP0] = jnp.concatenate(
+        [turned[...].T[:SHARD, 0:64].astype(bf16), wout_ref[...]], axis=1
+    )
+    pack_ref[:, DOWN0:WIDE] = wdown_ref[...]
+    pack_ref[:, UP0:DOWN0] = wup_ref[0]
+    pack_ref[:, Q0:KV0] = jnp.concatenate([wqkv_ref[0], jnp.zeros((SHARD, 64), bf16)], axis=1)
+    pack_ref[:, KV0:OUT0] = jnp.concatenate([wqkv_ref[1], wqkv_ref[2]], axis=1)
 
     def put(src, dst, send, recv, to, when=None):
         def make():
@@ -207,79 +222,89 @@
         return w_ref[l, :, :, :, :, first:last].reshape(D, last - first)
 
 
+    pieces = {"ud": (UP0, WIDE, UP0, 1), "qkv": (Q0, OUT0, 0, 0), "out": (OUT0, UP0, 0, 0)}
+    numbers = {"ud": 0, "qkv": 1, "out": 2}
     cin, s_out, zin, u_out, yin = (cin_b, cin_a), (s_b, s_a), (zin_b, zin_a), (u_b, u_a), (yin_b, yin_a)
 
-    def r_sems(l, half, i):
-        return r_send.at[2 * l + half, i], r_recv.at[2 * l + half, i]
+    def r_sems(l, piece, i):
+        return r_send.at[3 * l + numbers[piece], i], r_recv.at[3 * l + numbers[piece], i]
+
+    def spans(piece):
+        first, last, base, which = pieces[piece]
+        return pl.ds(first, last - first), pl.ds(first - base, last - first), which
 
     def keep_grad(l, first, value):
         n = value.shape[1]
         grads[l, :, :, :, :, first : first + n] = value.astype(bf16).reshape(4, 2, 2, SHARD, n)
 
-    def scatter_a(l, half):
-        put(grads.at[l, :, :, other, :, cols(half)], cin[half].at[l], *r_sems(l, half, 0), mate)
-
-    def scatter_b(l, half):
-        got(cin[half].at[l], *r_sems(l, half, 0))
+    def scatter_a(l, piece):
+        wide, span, n = spans(piece)
+        put(grads.at[l, :, :, other, :, wide], cin[n].at[l, :, :, :, span], *r_sems(l, piece, 0), mate)
+
+    def scatter_b(l, piece):
+        wide, span, n = spans(piece)
+        got(cin[n].at[l, :, :, :, span], *r_sems(l, piece, 0))
 
         def add(i, carry):
             for b in range(2):
-                s_out[half][l, i, b] = (
-                    grads[l, i, b, core, :, cols(half)].astype(f32) + cin[half][l, i, b].astype(f32)
+                s_out[n][l, i, b, :, span] = (
+                    grads[l, i, b, core, :, wide].astype(f32) + cin[n][l, i, b, :, span].astype(f32)
                 ).astype(bf16)
             return carry
 
         lax.fori_loop(0, 4, add, 0)
-        for d in (1, 3, 2):
-            put(s_out[half].at[l, :, lax.div(ring(z, d), 2)], zin[half].at[d - 1], *r_sems(l, half, d),
-                along_z(d), when=holds(l) if d == 2 else lacks(l))
-
-    def scatter_c(l, half):
+        for d in (2, 1, 3):
+            put(s_out[n].at[l, :, lax.div(ring(z, d), 2), :, span], zin[n].at[d - 1, :, :, span],
+                *r_sems(l, piece, d), along_z(d), when=holds(l) if d == 2 else lacks(l))
+
+    def scatter_c(l, piece):
+        wide, span, n = spans(piece)
+
         @pl.when(holds(l))
         def _():
             for d in (1, 3, 2):
-                got(zin[half].at[d - 1], *r_sems(l, half, d))
+                got(zin[n].at[d - 1, :, :, span], *r_sems(l, piece, d))
 
             def add(i, carry):
-                total = s_out[half][l, i, zh].astype(f32)
+                total = s_out[n][l, i, zh, :, span].astype(f32)
                 for d in (1, 2, 3):
-                    total = total + zin[half][d - 1, i].astype(f32)
-                u_out[half][i] = total.astype(bf16)
+                    total = total + zin[n][d - 1, i, :, span].astype(f32)
+                u_out[n][i, :, span] = total.astype(bf16)
                 return carry
 
             lax.fori_loop(0, 4, add, 0)
 
         for d in (2, 1, 3):
-            put(u_out[half].at[ring(y, d)], yin[half].at[d - 1], *r_sems(l, half, 3 + d), along_y(d),
-                when=holds(l))
-
-    def scatter_d(l, half):
+            put(u_out[n].at[ring(y, d), :, span], yin[n].at[d - 1, :, span], *r_sems(l, piece, 3 + d),
+                along_y(d), when=holds(l))
+
+    def scatter_d(l, piece):
+        wide, span, n = spans(piece)
+
         @pl.when(holds(l))
         def _():
-            total = u_out[half][y].astype(f32)
+            total = u_out[n][y, :, span].astype(f32)
             for d in (1, 3, 2):
-                got(yin[half].at[d - 1], *r_sems(l, half, 3 + d))
-                total = total + yin[half][d - 1].astype(f32)
-            own_ref[:, cols(half)] = total
-
-
-    h = lax.div(t, 2)
-
-    def place(l, kind):
-        to_z = h * 2 + l
-        dst = dist_ref.at[z, lax.rem(t, 2), kind]
-        for a in range(4):
-            here = jnp.logical_and(to_z == z, t == a)
-            put(kept.at[l, kind], dst, d_send.at[2 * l + kind, a], d_recv.at[z, lax.rem(t, 2), kind],
-                ident(y, to_z, core, a), when=jnp.logical_not(here))
-
-        def make():
-            return pltpu.make_async_copy(kept.at[l, kind], dst, d_local.at[kind])
-
-        pl.when(to_z == z)(lambda: make().start())
-        placed.append((to_z == z, make))
+                got(yin[n].at[d - 1, :, span], *r_sems(l, piece, 3 + d))
+                total = total + yin[n][d - 1, :, span].astype(f32)
+            own_ref[:, wide] = total
+
 
     placed = []
+
+    def place(l, kind, ref):
+        for half in range(2):
+            to_z = 2 * half + l
+            src = ref.at[pl.ds(half * BLOCK, BLOCK)]
+            dst = dist_ref.at[kind, z]
+            put(src, dst, d_send.at[2 * l + kind, half], d_recv.at[kind, z], ident(y, to_z, core, t),
+                when=z != to_z)
+            make = functools.partial(pltpu.make_async_copy, src, dst, d_local.at[kind])
+            start_here(z == to_z, make)
+            placed.append((z == to_z, make))
+
+    def start_here(when, make):
+        pl.when(when)(lambda: make().start())
 
 
     quarter = pl.ds(pl.multiple_of(t * QUARTER, QUARTER), QUARTER)
@@ -319,23 +344,33 @@
     def from_heads(rows, masks):
         return sum(rows[i * ROWS : (i + 1) * ROWS] * masks[i] for i in range(3))
 
+    length = len_ref[z, 0]
+    within = lax.broadcasted_iota(jnp.int32, (ROWS, 1), 0)
+    within = jnp.where(within >= BLOCK, within + BLOCK, within)
+
+    def masked(b, s):
+        first = (lax.div(b, 2) * 4 + lax.rem(b, 2)) * BLOCK
+        return jnp.where(within < length - first, s, negative)
+
     def key_rows(b):
         return pl.ds(pl.multiple_of(b * ROWS, ROWS), ROWS)
+
+    def send_keys(l):
+        own = kv.at[l, y * 2 + core]
+        for d in (1, 3, 2):
+            put(own, own, k_send.at[l, d - 1], k_recv.at[l, d - 1], along_y(d))
+        put(own, own, k_send.at[l, 3], k_recv.at[l, 3], mate)
 
     def attend(l, meanwhile):
         def sems(i):
             return k_send.at[l, i], k_recv.at[l, i]
 
         own = y * 2 + core
-        for d in (1, 3, 2):
-            put(kv.at[l, own], kv.at[l, own], *sems(d - 1), along_y(d))
-        put(kv.at[l, own], kv.at[l, own], *sems(3), mate)
-        meanwhile()
         q3 = by_head(q[l], q_masks).astype(bf16)
 
         def first(b, top):
             s = dot_t(kv[l, b, :, 0:256], q3)
-            s = jnp.where(keep_ref[key_rows(b), :] < 0, negative, s)
+            s = masked(b, s)
             scores[key_rows(b), :] = s
             return jnp.maximum(top, jnp.max(s, axis=0, keepdims=True))
 
@@ -362,6 +397,7 @@
             return first(b, top)
 
         top = lax.fori_loop(0, 3, other_core, top)
+        meanwhile()
         acc[...] = jnp.zeros_like(acc)
 
         def second(b, total):
@@ -386,7 +422,7 @@
 
         def block(b):
             k = kv[l, b, :, 0:256]
-            s = jnp.where(keep_ref[key_rows(b), :] < 0, negative, dot_t(k, q3))
+            s = masked(b, dot_t(k, q3))
             p = jnp.exp(s - log_total)
             ds = (p * (dot_t(kv[l, b, :, 128:384], do3) - delta)).astype(bf16)
             dk = dot(ds, q3)
@@ -394,15 +430,14 @@
             acc[...] += dot(k.T, ds)
             return jnp.concatenate([dk[:, :128], dk[:, 128:] + dv[:, :128], dv[:, 128:]], axis=1)
 
-        def for_mate(i, carry):
-            off = 3 - i
+        def for_mate(off):
             b = ring(y, off) * 2 + other
             dkv[l, b] = block(b).astype(bf16)
             remote(dkv.at[l, b], core_in.at[l, off], *sems(off), mate).start()
-            return carry
-
-        def for_y(i, carry):
-            off = 3 - i
+
+        def step(i, carry):
+            off = 2 + i - 3 * lax.div(i, 2)
+            for_mate(off)
             b = ring(y, off) * 2 + core
             value = block(b)
             got(core_in.at[l, off], *sems(off))
@@ -410,8 +445,8 @@
             remote(dkv.at[l, b], y_in.at[l, off - 1], *sems(3 + off), along_y(off)).start()
             return carry
 
-        lax.fori_loop(0, 4, for_mate, 0)
-        lax.fori_loop(0, 3, for_y, 0)
+        lax.fori_loop(0, 3, step, 0)
+        for_mate(0)
         for off in range(4):
             b = ring(y, off) * 2 + other
             later.append((None, functools.partial(remote, dkv.at[l, b], core_in.at[l, off], *sems(off), mate)))
@@ -436,9 +471,10 @@
     def forward(l, x_q, on_kv, on_sum, on_share, on_last):
         row = small[l]
         bias = dot(row.astype(bf16), sel_ref[...])
-        wide = dot(n1[l], weight(l, Q0, OUT0))
-        kv[l, y * 2 + core] = (wide[:, 256:] + bias[8:9, 256:]).astype(bf16)
-        q[l] = ((wide[:, :256] + bias[7:8, :256]).astype(bf16).astype(f32) * 0.125).astype(bf16)
+        kv[l, y * 2 + core] = (dot(n1[l], weight(l, KV0, OUT0)) + bias[8:9, 256:]).astype(bf16)
+        send_keys(l)
+        queries = dot(n1[l], weight(l, Q0, KV0)) + bias[7:8, :256]
+        q[l] = (queries.astype(bf16).astype(f32) * 0.125).astype(bf16)
         attend(l, on_kv)
         part[2 * l] = dot_t(att[l], weight(l, OUT0, UP0)).astype(bf16)
         sum_start(4 * l, 2 * l)
@@ -449,6 +485,7 @@
         share_start(4 * l + 1, n2.at[l])
         on_share()
         share_wait(4 * l + 1, n2.at[l])
+        gather_d(l, 1)
         u = dot(n2[l], weight(l, UP0, DOWN0)) + row[6:7]
         phi = 0.5 * (1.0 + lax.erf(u * np.float32(0.5**0.5)))
         act[l] = (u * phi).astype(bf16)
@@ -456,9 +493,7 @@
         sum_start(4 * l + 2, 2 * l + 1)
         slope[l] = phi + u * jnp.exp(-0.5 * u * u) * np.float32((2 * np.pi) ** -0.5)
         on_last()
-        out = m + sum_wait(4 * l + 2, 2 * l + 1) + row[5:6]
-        kept[l, 0] = out.astype(bf16)
-        return out
+        return (m + sum_wait(4 * l + 2, 2 * l + 1) + row[5:6]).astype(bf16)
 
     def backward(l, dout_q, gdi_ref, x_q, on_sum, on_share, on_att, on_last):
         base = 8 + 4 * (1 - l)
@@ -488,23 +523,22 @@
         part[5 + 2 * l] = dot_t(dqkv[l], weight(l, Q0, OUT0)).astype(bf16)
         sum_start(base + 2, 5 + 2 * l)
         keep_grad(l, Q0, dot(n1[l].T, dqkv[l]))
+        scatter_a(l, "qkv")
         sums = jnp.sum(dqkv[l].astype(f32), axis=0, keepdims=True)
         wide_col = lax.broadcasted_iota(jnp.int32, (8, 640), 1)
         which = lax.broadcasted_iota(jnp.int32, (8, 640), 0)
         two = jnp.where(((wide_col < 256) & (which == 0)) | ((wide_col >= 256) & (which == 1)), sums, 0.0)
         placed_rows = dot_t(two.astype(bf16), sel_ref[...])
         little[l, 7:9, :] = placed_rows[0:2]
+        both[...] = dot(ga[l].T, att[l])
         on_last()
         c = sum_wait(base + 2, 5 + 2 * l)
         gv, g_gain, g_shift = norm_back(x_q, row[0:1], c)
         little[l, 0:1, :] = g_gain
         little[l, 2:3, :] = g_shift
-        gx = gm + gv
-        kept[l, 1] = gx.astype(bf16)
-        return gx
+        return (gm + gv).astype(bf16)
 
     def out_grads(l):
-        both = dot(ga[l].T, att[l])
         keep_grad(l, OUT0, jnp.concatenate([both[:, :128] + little[l].T, both[:, 128:]], axis=1))
 
 
@@ -513,19 +547,20 @@
     twin = ident(y, 3 - z, core, t)
     mine = pl.ds(pl.multiple_of(zh * BLOCK, BLOCK), BLOCK)
     theirs = pl.ds(pl.multiple_of((1 - zh) * BLOCK, BLOCK), BLOCK)
-    put(f_ref.at[3 - z], x_all.at[mine], f_send.at[0], f_recv.at[0], twin)
+    put(f_ref.at[3 - z, 0], x_all.at[mine], f_send.at[0], f_recv.at[0], twin)
+    row, column = (lax.broadcasted_iota(jnp.int32, (SHARD, 640), i) for i in range(2))
+    for i in range(16):
+        hit = ((column == row + 12 * i) | (column == row + 12 * i + 448)) & (row < 12)
+        sel_ref[i * SHARD : (i + 1) * SHARD, :] = jnp.where(hit, 1.0, 0.0).astype(bf16)
+    x_all[mine, :] = f_ref[z, 0]
+    g_all[mine, :] = og_ref[z, 0]
+    gather_b(0, B)
     gather_a(0, A)
-    put(og_ref.at[3 - z], g_all.at[mine], f_send.at[1], f_recv.at[1], twin)
-    x_all[mine, :] = f_ref[z]
-    g_all[mine, :] = og_ref[z]
-    gather_b(0, B)
+    put(og_ref.at[3 - z, 0], g_all.at[mine], f_send.at[1], f_recv.at[1], twin)
     gather_c(0, B)
-    gather_b(0, A)
     got(x_all.at[theirs], f_send.at[0], f_recv.at[0])
     gather_d(0, B)
     load_small(0)
-    n1[0] = norm(x_all[...].astype(f32), small[0, 0:1, :], small[0, 2:3, :]).astype(bf16)
-    x0 = x_all[quarter, :].astype(f32)
 
     def run(*steps):
         def body():
@@ -534,43 +569,58 @@
 
         return body
 
-    x1 = forward(
+    def start_layer(l, ref):
+        n1[l] = norm(ref[...].astype(f32), small[l, 0:1, :], small[l, 2:3, :]).astype(bf16)
+        return ref[quarter, :].astype(f32)
+
+    x0 = start_layer(0, x_all)
+    x1_all[quarter, :] = forward(
         0, x0,
-        run((gather_c, 0, A), (gather_a, 1, B), (gather_a, 1, A)),
-        run((gather_d, 0, A), (gather_b, 1, B)),
-        run((gather_b, 1, A)),
-        run((gather_c, 1, B), (gather_c, 1, A)),
-    ).astype(bf16).astype(f32)
+        run((gather_b, 0, A)),
+        run((gather_a, 1, B), (gather_a, 1, A)),
+        run((gather_c, 0, A)),
+        run((gather_b, 1, B)),
+    )
+    share_start(3, x1_all)
+    gather_c(1, B)
+    share_wait(3, x1_all)
     gather_d(1, B)
     load_small(1)
-    n1[1, quarter, :] = norm(x1, small[1, 0:1, :], small[1, 2:3, :]).astype(bf16)
-    share_start(3, n1.at[1])
-    share_wait(3, n1.at[1])
-    forward(1, x1, run((place, 0, 0)), run((gather_d, 1, A)), run(), run())
+    x1 = start_layer(1, x1_all)
+    o1_all[quarter, :] = forward(
+        1, x1, run((gather_b, 1, A)), run((place, 0, 0, x1_all)), run((gather_c, 1, A)), run()
+    )
     got(g_all.at[theirs], f_send.at[1], f_recv.at[1])
-    gx = backward(
+    gx1_all[quarter, :] = backward(
         1, g_all[quarter, :].astype(f32), g_all, x1,
-        run((scatter_a, 1, A)), run((scatter_b, 1, A)), run((place, 1, 0)), run((scatter_c, 1, A)),
-    ).astype(bf16)
-    gdi0[quarter, :] = gx
-    share_start(11, gdi0)
+        run((scatter_a, 1, "ud")), run((scatter_b, 1, "ud")), run((share_start, 7, o1_all)),
+        run((scatter_c, 1, "ud")),
+    )
+    share_start(11, gx1_all)
     out_grads(1)
-    scatter_a(1, B)
-    share_wait(11, gdi0)
-    backward(
-        0, gx.astype(f32), gdi0, x0,
-        run((scatter_a, 0, A), (scatter_b, 1, B)), run((scatter_b, 0, A)), run((place, 1, 1)),
-        run((scatter_c, 0, A), (scatter_c, 1, B)),
+    scatter_a(1, "out")
+    scatter_b(1, "qkv")
+    share_wait(11, gx1_all)
+    gx0_all[quarter, :] = backward(
+        0, gx1_all[quarter, :].astype(f32), gx1_all, x0,
+        run((scatter_a, 0, "ud"), (scatter_b, 1, "out")),
+        run((scatter_b, 0, "ud")),
+        run((place, 1, 1, gx1_all), (share_wait, 7, o1_all), (place, 1, 0, o1_all)),
+        run((scatter_c, 1, "qkv"), (scatter_c, 1, "out"), (scatter_c, 0, "ud"), (scatter_b, 0, "qkv")),
     )
     out_grads(0)
-    scatter_a(0, B)
-    place(0, 1)
-    scatter_d(1, A)
-    scatter_d(0, A)
-    scatter_b(0, B)
-    scatter_d(1, B)
-    scatter_c(0, B)
-    scatter_d(0, B)
+    scatter_a(0, "out")
+    share_start(15, gx0_all)
+    for piece in ("ud", "qkv", "out"):
+        scatter_d(1, piece)
+    scatter_c(0, "qkv")
+    scatter_b(0, "out")
+    scatter_d(0, "ud")
+    share_wait(15, gx0_all)
+    place(0, 1, gx0_all)
+    scatter_c(0, "out")
+    scatter_d(0, "qkv")
+    scatter_d(0, "out")
     tiles[0] = own_ref[:, OUT0 : OUT0 + 128]
     for d in (1, 2, 3):
         put(tiles.at[0], tiles.at[d], t_send.at[d - 1], t_recv.at[d - 1], along_x(d))
@@ -581,12 +631,10 @@
     tile_ref[...] = tile
     for kind in range(2):
         for zz in range(4):
-            for b in range(2):
-                away = jnp.logical_not(jnp.logical_and(zz == z, t == zh * 2 + b))
-
-                @pl.when(away)
-                def _():
-                    got(dist_ref.at[zz, b, kind], d_send.at[0, 0], d_recv.at[zz, b, kind])
+
+            @pl.when(z != zz)
+            def _():
+                got(dist_ref.at[kind, zz], d_send.at[0, 0], d_recv.at[kind, zz])
 
     for when, make in placed:
         pl.when(when)(lambda: make().wait())
@@ -597,7 +645,7 @@
             pl.when(when)(lambda: make().wait_send())
 
 
-def layers_call(packed, frames, out_grad, keep, sel):
+def layers_call(*arrays):
     vmem = pl.BlockSpec(memory_space=pltpu.VMEM)
     wide_a, wide_b = WIDE - UP0, UP0
     dma = pltpu.SemaphoreType.DMA
@@ -606,19 +654,25 @@
         out_shape=(
             jax.ShapeDtypeStruct((SHARD, WIDE), f32),
             jax.ShapeDtypeStruct((SHARD, 128), f32),
-            jax.ShapeDtypeStruct((4, 2, 2, QUARTER, D), bf16),
+            jax.ShapeDtypeStruct((2, 4, BLOCK, D), bf16),
         ),
-        in_specs=[vmem] * 5,
+        in_specs=[vmem] * 9 + [pl.BlockSpec(memory_space=pltpu.SMEM)] + [vmem],
         out_specs=(vmem, vmem, pl.BlockSpec(memory_space=pl.ANY)),
         scratch_shapes=[
+            pltpu.VMEM((SHARD, WIDE), bf16),
+            pltpu.VMEM((128, 128), f32),
+            pltpu.VMEM((D, 640), bf16),
             pltpu.VMEM((2, 4, 2, 2, SHARD, WIDE), bf16),
             pltpu.VMEM((2, 4, 2, 2, SHARD, WIDE), bf16),
             pltpu.VMEM((ROWS, D), bf16),
             pltpu.VMEM((ROWS, D), bf16),
-            pltpu.VMEM((2, 2, QUARTER, D), bf16),
+            pltpu.VMEM((ROWS, D), bf16),
+            pltpu.VMEM((ROWS, D), bf16),
+            pltpu.VMEM((ROWS, D), bf16),
+            pltpu.VMEM((ROWS, D), bf16),
+            pltpu.VMEM((D, 256), f32),
             pltpu.VMEM((2, ROWS, D), bf16),
             pltpu.VMEM((2, ROWS, D), bf16),
-            pltpu.VMEM((ROWS, D), bf16),
             pltpu.VMEM((2, ROWS, D), bf16),
             pltpu.VMEM((8, 3, QUARTER, D), bf16),
             pltpu.VMEM((8, ROWS, D), bf16),
@@ -652,62 +706,32 @@
             dma((2, 7)), dma((2, 7)),
             dma((2, 7)), dma((2, 7)),
             dma((4, 7)), dma((4, 7)),
-            dma((4, 7)), dma((4, 7)),
+            dma((6, 7)), dma((6, 7)),
             dma((2,)), dma((2,)),
-            dma((4, 4)), dma((4, 2, 2)), dma((2,)),
+            dma((4, 2)), dma((2, 4)), dma((2,)),
             dma((3,)), dma((3,)),
         ],
         compiler_params=pltpu.CompilerParams(
             collective_id=0, has_side_effects=True, vmem_limit_bytes=VMEM_LIMIT
         ),
         name="layers",
-    )(packed, frames, out_grad, keep, sel)
-
-
-def selection():
-    sel = np.zeros((D, 640), np.float32)
-    for c in range(16):
-        for i in range(12):
-            sel[c * 48 + i, c * 12 + i] = 1.0
-            sel[c * 48 + i, 448 + c * 12 + i] = 1.0
-    return sel
-
-
-def key_frames():
-    r = np.arange(KEYS)
-    j, w = r // ROWS, r % ROWS
-    y, core = j // 2, j % 2
-    hi = w // BLOCK
-    return (((y * 2 + hi) * 2 + core) * BLOCK + w % BLOCK).astype(np.int32)
+    )(*arrays)
 
 
 def on_device(
     frames, w_qkv, w_out, w_up, w_down, ln_gains, shifts, qv_bias, up_bias, lengths, out_grad
 ):
-    _, z, _, _ = where_am_i()
-    pad = ((0, 0), (0, SHARD - 12))
-    little = jnp.concatenate(
-        [ln_gains[0], shifts[0], up_bias, jnp.pad(qv_bias[0], pad), jnp.zeros((55, SHARD), bf16)], axis=0
-    )
-    packed = jnp.concatenate(
-        [
-            w_qkv[0, :, 0], jnp.zeros((SHARD, 64), bf16), w_qkv[0, :, 1], w_qkv[0, :, 2],
-            little.T, w_out[0].T, w_up[0], w_down[0].T,
-        ],
-        axis=1,
-    )
-    length = lax.dynamic_index_in_dim(lengths, z, 0, keepdims=False)[0]
-    keep = jnp.where(jnp.asarray(key_frames())[:, None] < length, 0.0, -1.0).astype(f32)
     own, tile, dist = layers_call(
-        packed, frames[:, 0], out_grad[:, 0], keep, jnp.asarray(selection(), bf16)
+        frames, jnp.transpose(w_qkv[0], (1, 0, 2)), w_out[0].T, w_up, w_down[0].T, ln_gains, shifts, qv_bias,
+        up_bias, lengths, out_grad,
     )
     outs = dist.astype(f32)
     tile_t = tile.T
     little_t = own[:, OUT0 : OUT0 + 64].T
     grad_qkv = jnp.stack([own[:, 0:192], own[:, 256:448], own[:, 448:640]], axis=1)
     return (
-        outs[:, :, 0].reshape(1, 4, 1, BLOCK, D),
-        outs[:, :, 1].reshape(1, 4, 1, BLOCK, D),
+        outs[0].reshape(1, 4, 1, BLOCK, D),
+        outs[1].reshape(1, 4, 1, BLOCK, D),
         grad_qkv[None],
         own[:, OUT0 + 64 : UP0].T[None],
         own[:, UP0:DOWN0][None],

time: 225 us -> 203 us (0.902); the launches traced: 224 us -> 199 us
  Pallas kernels: 207 us -> 189 us
  local copies, waits for them, and re-layouts: 14.5 us -> 7.06 us
    pallas_call x1, Pallas kernels: 207 us -> 189 us  [layers_call(): pl.pallas_call(layers_kernel, out_shape=(jax.ShapeDtypeStruct((SHARD, WID...]
    slice x1 -> x0, local copies, waits for them, and re-layouts: 2.95 us -> none  [on_device(): outs[:, :, 1].reshape(1, 4, 1, BLOCK, D)]
    squeeze x3 -> x0, local copies, waits for them, and re-layouts: 2.28 us -> none  [the longest x1 0.78 us: on_device(): w_qkv[0, :, 2]]
where the time goes in v3:
time: 203 us; the launch traced here: 199 us
  Pallas kernels  189 us (93%)
  local copies, waits for them, and re-layouts  7.06 us (3%)
  other arithmetic  2.14 us (1%)
    pallas_call x1, Pallas kernels, layers_call(): pl.pallas_call(layers_kernel, out_shape=(jax.ShapeDtypeStruct((SHARD, WID...  189 us
    unnamed x8, local copies, waits for them, and re-layouts  4.12 us

profile of v3, /device:TPU:1, one launch (start us, length us, event | category | flops | bytes accessed | tf_op | source)
XLA Modules:
  0.0 199.3 jit_solution(10369604429148283104)
XLA Ops:
  0.6 1.3 copy.21.len_ref
  2.0 189.4 %layers.1 = (f32[48,2432]{1,0:T(8,128)}, f32[48,128]{1,0:T(8,128)}, bf16[2,4,96,768]{3,2,1,0:T(8,128)(2,1)}) custom-call(bf16[4,1,96,768]{3,2,1,0:T(8,128)(2,1)} %f_ref.1, bf16[3,48,192]{2,1,0:T(8,128)(2,1)} %bitcast.45, bf16[48,192]{1,0:T(8,128)(2,1)} %bitcast.47, bf16[1,48,768]{2,1,0:T(8,128)(2,1)} %wup_ref.1, bf16[48,768]{1,0:T(8,128)(2,1)} %bitcast.46, ...), custom_call_target="tpu_custom_call" | custom-call | tf_op jit(solution)/shard_map/layers/pallas_call | solution.py:652
  191.4 1.5 convert_element_type.3
  192.9 0.0 copy-start
  192.9 1.6 slice_bitcast_fusion
  194.4 0.0 copy-start.1
  194.4 0.0 copy-done
  194.4 0.7 slice_bitcast_fusion.4
  195.1 0.7 maximum_bitcast_fusion
  195.8 0.7 slice_bitcast_fusion.2
  196.5 0.0 copy-done.1
  196.5 0.6 copy.22
  197.2 0.1 slice_bitcast_fusion.8
  197.2 0.7 copy.26
  197.9 0.1 slice.56
  198.0 0.7 copy.23
  198.6 0.1 slice.57
  198.7 0.6 copy.27
  (1 shorter events, 0.0 us)
Async XLA Ops:
  192.9 1.6 copy-start
  194.4 2.1 %copy-start.1 = (f32[48,128]{1,0:T(8,128)S(1)}, f32[48,128]{1,0:T(8,128)}, u32[]{:S(2)}) copy-start(f32[48,128]{1,0:T(8,128)} %get-tuple-element.15) | copy-start | bytes 73732

commit v4 on v3

--- a/solution.py
+++ b/solution.py
@@ -21,9 +21,7 @@
 ROWS = 192
 KEYS = 1536
 Q0, KV0, OUT0, UP0, DOWN0, WIDE = 0, 256, 640, 896, 1664, 2432
-HALF = 1280
-PIECE = 256
-HEADS3 = 3
+GROUPS = ((0, 48),)
 VMEM_LIMIT = 60 * 1024 * 1024
 
 
@@ -87,12 +85,12 @@
 
 def layers_kernel(
     f_ref, wqkv_ref, wout_ref, wup_ref, wdown_ref, gains_ref, shifts_ref, qv_ref, up_ref, len_ref, og_ref,
-    own_ref, tile_ref, dist_ref,
-    pack_ref, turned, sel_ref, w_ref, grads, x_all, g_all, x1_all, o1_all, gx1_all, gx0_all, both, n1, n2, ga, rs, part, kv, att, act, slope, mid, lse, q, small,
+    own_ref, small_ref, dist_ref,
+    pack_ref, turned, sel_ref, w_ref, grads, x_all, g_all, x1_all, o1_all, gx1_all, gx0_all, both, gpre, gatt, gout, gmid, wo, att_all, m_all, n1, n2, ga, rs, part, kv, att, act, slope, mid, lse, q, small,
     scores, acc, dkv, dqkv, core_in, y_in, little,
     cin_a, cin_b, s_a, s_b, zin_a, zin_b, u_a, u_b, yin_a, yin_b, tiles,
     x_send, x_recv, k_send, k_recv, b_send, b_recv, w_send, w_recv, r_send, r_recv, f_send, f_recv,
-    d_send, d_recv, d_local, t_send, t_recv,
+    d_send, d_recv, d_local, t_send, t_recv, o_send, o_recv,
 ):
     y, z, core, t = where_am_i()
     other = 1 - core
@@ -140,12 +138,25 @@
             pl.when(when)(lambda: make().start())
         later.append((when, make))
 
+    marks = [0, 0]
+
+    def drain():
+        n = marks.pop(0)
+        for when, make in later[:n]:
+            if when is None:
+                make().wait_send()
+            else:
+                pl.when(when)(lambda make=make: make().wait_send())
+        del later[:n]
+        marks[:] = [m - n for m in marks] + [len(later)]
+
     def got(region, send, recv):
         remote(region, region, send, recv, mate).wait_recv()
 
 
     def cols(half):
-        return pl.ds(0, UP0) if half == 0 else pl.ds(UP0, WIDE - UP0)
+        first, last = ((0, UP0), (UP0, DOWN0), (DOWN0, WIDE))[half]
+        return pl.ds(first, last - first)
 
     first_core, second_core = core == 0, core == 1
 
@@ -156,7 +167,7 @@
         return lax.rem(z, 2) != l
 
     def w_sems(l, half, i):
-        return w_send.at[2 * l + half, i], w_recv.at[2 * l + half, i]
+        return w_send.at[3 * l + half, i], w_recv.at[3 * l + half, i]
 
     def gather_a(l, half):
         here = w_ref.at[l, y, zh, core, :, cols(half)]
@@ -217,6 +228,28 @@
 
     def gather_d(l, half):
         got(w_ref.at[l, :, :, other, :, cols(half)], *w_sems(l, half, 6))
+
+
+    def out_sems(l, i):
+        return o_send.at[l, i], o_recv.at[l, i]
+
+    def fetch_out(l):
+        src = w_ref.at[l, :, :, core, :, pl.ds(OUT0, UP0 - OUT0)]
+        for d in (1, 3, 2):
+            put(src, wo.at[l, t, :, :, core], *out_sems(l, d - 1), along_x(d))
+
+    def pass_out(l):
+        for d in (1, 3, 2):
+            mine = wo.at[l, ring(t, 4 - d), :, :, core]
+            got(mine, *out_sems(l, d - 1))
+            put(mine, mine, *out_sems(l, 2 + d), mate)
+
+    def have_out(l):
+        for d in (1, 3, 2):
+            got(wo.at[l, ring(t, 4 - d), :, :, other], *out_sems(l, 2 + d))
+
+    def out_weight(l, i):
+        return wo[l, i].reshape(D, UP0 - OUT0)
 
     def weight(l, first, last):
         return w_ref[l, :, :, :, :, first:last].reshape(D, last - first)
@@ -307,30 +340,49 @@
         pl.when(when)(lambda: make().start())
 
 
-    quarter = pl.ds(pl.multiple_of(t * QUARTER, QUARTER), QUARTER)
-
-    def rows_of(i):
-        return pl.ds(pl.multiple_of(i * QUARTER, QUARTER), QUARTER)
-
-    def share_start(phase, ref):
-        for d in (1, 3, 2):
-            put(ref.at[quarter], ref.at[quarter], x_send.at[phase, d - 1], x_recv.at[phase, d - 1], along_x(d))
-
-    def share_wait(phase, ref):
-        for d in (1, 3, 2):
-            got(ref.at[rows_of(ring(t, 4 - d))], x_send.at[phase, d - 1], x_recv.at[phase, d - 1])
-
-    def sum_start(phase, i):
-        for d in (1, 3, 2):
-            put(part.at[i, rows_of(ring(t, d))], rs.at[i, d - 1], x_send.at[phase, d - 1],
-                x_recv.at[phase, d - 1], along_x(d))
-
-    def sum_wait(phase, i):
-        total = part[i, quarter, :].astype(f32)
-        for d in (1, 3, 2):
-            got(rs.at[i, d - 1], x_send.at[phase, d - 1], x_recv.at[phase, d - 1])
-            total = total + rs[i, d - 1].astype(f32)
+    def group(g):
+        return slice(g[0], g[0] + 4 * g[1])
+
+    def rows_of(g, i):
+        return pl.ds(pl.multiple_of(g[0] + i * g[1], 16), g[1])
+
+    def own_rows(g):
+        return rows_of(g, t)
+
+    def packed_rows(g):
+        return slice(g[0] // 4, g[0] // 4 + g[1])
+
+    def x_sems(phase, g, d):
+        i = GROUPS.index(g) * 3 + d - 1
+        return x_send.at[phase, i], x_recv.at[phase, i]
+
+    def share_start(phase, ref, g):
+        for d in (1, 3, 2):
+            put(ref.at[own_rows(g)], ref.at[own_rows(g)], *x_sems(phase, g, d), along_x(d))
+
+    def share_wait(phase, ref, g):
+        for d in (1, 3, 2):
+            got(ref.at[rows_of(g, ring(t, 4 - d))], *x_sems(phase, g, d))
+
+    def sum_start(phase, i, g):
+        at = pl.ds(g[0] // 4, g[1])
+        for d in (1, 3, 2):
+            put(part.at[i, rows_of(g, ring(t, d))], rs.at[i, d - 1, at], *x_sems(phase, g, d), along_x(d))
+
+    def sum_wait(phase, i, g):
+        total = part[i, own_rows(g), :].astype(f32)
+        for d in (1, 3, 2):
+            got(rs.at[i, d - 1, pl.ds(g[0] // 4, g[1])], *x_sems(phase, g, d))
+            total = total + rs[i, d - 1, packed_rows(g), :].astype(f32)
         return total
+
+    def share_all(phase, ref):
+        for g in GROUPS:
+            share_start(phase, ref, g)
+
+    def shared_all(phase, ref):
+        for g in GROUPS:
+            share_wait(phase, ref, g)
 
 
     col = lax.broadcasted_iota(jnp.int32, (1, 256), 1)
@@ -344,7 +396,7 @@
     def from_heads(rows, masks):
         return sum(rows[i * ROWS : (i + 1) * ROWS] * masks[i] for i in range(3))
 
-    length = len_ref[z, 0]
+    length = len_ref[0, z]
     within = lax.broadcasted_iota(jnp.int32, (ROWS, 1), 0)
     within = jnp.where(within >= BLOCK, within + BLOCK, within)
 
@@ -355,11 +407,18 @@
     def key_rows(b):
         return pl.ds(pl.multiple_of(b * ROWS, ROWS), ROWS)
 
-    def send_keys(l):
-        own = kv.at[l, y * 2 + core]
-        for d in (1, 3, 2):
-            put(own, own, k_send.at[l, d - 1], k_recv.at[l, d - 1], along_y(d))
-        put(own, own, k_send.at[l, 3], k_recv.at[l, 3], mate)
+    def k_sems(l, i):
+        return k_send.at[l, i], k_recv.at[l, i]
+
+    def key_part(l, b, g):
+        return kv.at[l, b, pl.ds(g[0], 4 * g[1])]
+
+    def send_keys(l, g):
+        own = key_part(l, y * 2 + core, g)
+        i = GROUPS.index(g)
+        for d in (1, 3, 2):
+            put(own, own, *k_sems(l, 3 * i + d - 1), along_y(d))
+        put(own, own, *k_sems(l, 6 + i), mate)
 
     def attend(l, meanwhile):
         def sems(i):
@@ -375,25 +434,27 @@
             return jnp.maximum(top, jnp.max(s, axis=0, keepdims=True))
 
         top = first(own, jnp.full((1, 3 * ROWS), negative, f32))
-        got(kv.at[l, y * 2 + other], *sems(3))
+        for i, g in enumerate(GROUPS):
+            got(key_part(l, y * 2 + other, g), *sems(6 + i))
         top = first(y * 2 + other, top)
 
         def same_core(i, top):
             d = 1 + 2 * i - 3 * lax.div(i, 2)
             b = ring(y, 4 - d) * 2 + core
-            got(kv.at[l, b], *sems(d - 1))
-            remote(kv.at[l, b], kv.at[l, b], *sems(3 + d), mate).start()
+            for j, g in enumerate(GROUPS):
+                got(key_part(l, b, g), *sems(3 * j + d - 1))
+            remote(kv.at[l, b], kv.at[l, b], *sems(7 + d), mate).start()
             return first(b, top)
 
         top = lax.fori_loop(0, 3, same_core, top)
         for d in (1, 2, 3):
             b = ring(y, 4 - d) * 2 + core
-            later.append((None, functools.partial(remote, kv.at[l, b], kv.at[l, b], *sems(3 + d), mate)))
+            later.append((None, functools.partial(remote, kv.at[l, b], kv.at[l, b], *sems(7 + d), mate)))
 
         def other_core(i, top):
             d = 1 + 2 * i - 3 * lax.div(i, 2)
             b = ring(y, 4 - d) * 2 + other
-            got(kv.at[l, b], *sems(3 + d))
+            got(kv.at[l, b], *sems(7 + d))
             return first(b, top)
 
         top = lax.fori_loop(0, 3, other_core, top)
@@ -408,6 +469,17 @@
         total = lax.fori_loop(0, 8, second, jnp.zeros((1, 3 * ROWS), f32))
         lse[l] = top + jnp.log(total)
         att[l] = from_heads((acc[...] / total).T, v_masks).astype(bf16)
+
+    def prepare(l):
+        q3 = by_head(q[l], q_masks).astype(bf16)
+        log_total = lse[l]
+
+        def step(b, carry):
+            s = scores[key_rows(b), :] if l == 1 else masked(b, dot_t(kv[l, b, :, 0:256], q3))
+            scores[key_rows(b), :] = jnp.exp(s - log_total)
+            return carry
+
+        lax.fori_loop(0, 8, step, 0)
 
     def attend_back(l, grad_att, meanwhile):
         def sems(i):
@@ -418,12 +490,10 @@
         delta = jnp.sum((do3 * by_head(att[l], v_masks)).T, axis=0, keepdims=True)
         do3 = do3.astype(bf16)
         acc[...] = jnp.zeros_like(acc)
-        log_total = lse[l]
 
         def block(b):
             k = kv[l, b, :, 0:256]
-            s = masked(b, dot_t(k, q3))
-            p = jnp.exp(s - log_total)
+            p = scores[key_rows(b), :]
             ds = (p * (dot_t(kv[l, b, :, 128:384], do3) - delta)).astype(bf16)
             dk = dot(ds, q3)
             dv = dot(p.astype(bf16), do3)
@@ -468,60 +538,106 @@
     def load_small(l):
         small[l] = weight(l, OUT0, OUT0 + 128).astype(f32).T[:16]
 
-    def forward(l, x_q, on_kv, on_sum, on_share, on_last):
+    def forward(l, x_ref, x_phase, out_ref, out_phase, on_kv, on_sum, on_share, on_last):
         row = small[l]
         bias = dot(row.astype(bf16), sel_ref[...])
-        kv[l, y * 2 + core] = (dot(n1[l], weight(l, KV0, OUT0)) + bias[8:9, 256:]).astype(bf16)
-        send_keys(l)
+        for g in GROUPS:
+            if x_phase is not None:
+                share_wait(x_phase, x_ref, g)
+            at = group(g)
+            n1[l, at, :] = norm(x_ref[at, :].astype(f32), row[0:1], row[2:3]).astype(bf16)
+            keys = dot(n1[l, at, :], weight(l, KV0, OUT0)) + bias[8:9, 256:]
+            kv[l, y * 2 + core, at, :] = keys.astype(bf16)
+            send_keys(l, g)
+        if l == 1:
+            fetch_out(l)
         queries = dot(n1[l], weight(l, Q0, KV0)) + bias[7:8, :256]
         q[l] = (queries.astype(bf16).astype(f32) * 0.125).astype(bf16)
         attend(l, on_kv)
-        part[2 * l] = dot_t(att[l], weight(l, OUT0, UP0)).astype(bf16)
-        sum_start(4 * l, 2 * l)
+        for d in (1, 3, 2):
+            put(att.at[l], att_all.at[l, t], *x_sems(4 * l, GROUPS[0], d), along_x(d))
+        m = x_ref[...].astype(f32) + dot_t(att[l], weight(l, OUT0, UP0)) + row[4:5]
         on_sum()
-        m = x_q + sum_wait(4 * l, 2 * l) + row[4:5]
-        mid[l] = m
-        n2[l, quarter, :] = norm(m, row[1:2], row[3:4]).astype(bf16)
-        share_start(4 * l + 1, n2.at[l])
+        drain()
+        have_out(l)
+        for d in (1, 3, 2):
+            i = ring(t, 4 - d)
+            got(att_all.at[l, i], *x_sems(4 * l, GROUPS[0], d))
+            m = m + dot_t(att_all[l, i], out_weight(l, i))
+        m_all[...] = m
+        n2[l] = norm(m, row[1:2], row[3:4]).astype(bf16)
         on_share()
-        share_wait(4 * l + 1, n2.at[l])
-        gather_d(l, 1)
-        u = dot(n2[l], weight(l, UP0, DOWN0)) + row[6:7]
-        phi = 0.5 * (1.0 + lax.erf(u * np.float32(0.5**0.5)))
-        act[l] = (u * phi).astype(bf16)
-        part[2 * l + 1] = dot_t(act[l], weight(l, DOWN0, WIDE)).astype(bf16)
-        sum_start(4 * l + 2, 2 * l + 1)
-        slope[l] = phi + u * jnp.exp(-0.5 * u * u) * np.float32((2 * np.pi) ** -0.5)
+        for g in GROUPS:
+            mid[l, packed_rows(g), :] = m_all[own_rows(g), :]
+        kept = []
+        for g in GROUPS:
+            at = group(g)
+            if g is GROUPS[0]:
+                gather_d(l, 1)
+            u = dot(n2[l, at, :], weight(l, UP0, DOWN0)) + row[6:7]
+            phi = 0.5 * (1.0 + lax.erf(u * np.float32(0.5**0.5)))
+            act[l, at, :] = (u * phi).astype(bf16)
+            gather_d(l, 2)
+            part[2 * l + 1, at, :] = dot_t(act[l, at, :], weight(l, DOWN0, WIDE)).astype(bf16)
+            sum_start(4 * l + 2, 2 * l + 1, g)
+            kept.append((at, u, phi))
+        for at, u, phi in kept:
+            slope[l, at, :] = phi + u * jnp.exp(-0.5 * u * u) * np.float32((2 * np.pi) ** -0.5)
         on_last()
-        return (m + sum_wait(4 * l + 2, 2 * l + 1) + row[5:6]).astype(bf16)
-
-    def backward(l, dout_q, gdi_ref, x_q, on_sum, on_share, on_att, on_last):
+        drain()
+        for g in GROUPS:
+            out = mid[l, packed_rows(g), :] + sum_wait(4 * l + 2, 2 * l + 1, g) + row[5:6]
+            out_ref[own_rows(g), :] = out.astype(bf16)
+            if out_phase is not None:
+                share_start(out_phase, out_ref, g)
+
+    def backward(l, d_ref, d_phase, x_ref, out_ref, out_phase, on_sum, on_share, on_att, on_last):
         base = 8 + 4 * (1 - l)
         row = small[l]
-        gdi = gdi_ref[...]
-        gpre = (dot(gdi, weight(l, DOWN0, WIDE)) * slope[l]).astype(bf16)
-        part[4 + 2 * l] = dot_t(gpre, weight(l, UP0, DOWN0)).astype(bf16)
-        sum_start(base, 4 + 2 * l)
-        keep_grad(l, UP0, dot(n2[l].T, gpre))
-        keep_grad(l, DOWN0, dot(gdi.T, act[l]))
         little[l] = jnp.zeros_like(little[l])
-        little[l, 6:7, :] = jnp.sum(gpre.astype(f32), axis=0, keepdims=True)
-        little[l, 5:6, :] = jnp.sum(dout_q, axis=0, keepdims=True)
+
+        def note(i, value):
+            little[l, i : i + 1, :] = little[l, i : i + 1, :] + jnp.sum(value, axis=0, keepdims=True)
+
+        for g in GROUPS:
+            at = group(g)
+            if d_phase is not None:
+                share_wait(d_phase, d_ref, g)
+            gpre[at, :] = (dot(d_ref[at, :], weight(l, DOWN0, WIDE)) * slope[l, at, :]).astype(bf16)
+            part[4 + 2 * l, at, :] = dot_t(gpre[at, :], weight(l, UP0, DOWN0)).astype(bf16)
+            sum_start(base, 4 + 2 * l, g)
+        keep_grad(l, UP0, dot(n2[l].T, gpre[...]))
+        keep_grad(l, DOWN0, dot(d_ref[...].T, act[l]))
+        note(6, gpre[...].astype(f32))
         on_sum()
-        c = sum_wait(base, 4 + 2 * l)
-        gv, g_gain, g_shift = norm_back(mid[l], row[1:2], c)
-        gm = dout_q + gv
-        low = gm.astype(bf16)
-        ga[l, quarter, :] = low
-        share_start(base + 1, ga.at[l])
-        little[l, 1:2, :] = g_gain
-        little[l, 3:4, :] = g_shift
-        little[l, 4:5, :] = jnp.sum(low.astype(f32), axis=0, keepdims=True)
+        drain()
+        for g in GROUPS:
+            c = sum_wait(base, 4 + 2 * l, g)
+            dout = d_ref[own_rows(g), :].astype(f32)
+            gv, g_gain, g_shift = norm_back(mid[l, packed_rows(g), :], row[1:2], c)
+            gm = dout + gv
+            low = gm.astype(bf16)
+            gmid[packed_rows(g), :] = gm
+            ga[l, own_rows(g), :] = low
+            for d in (2, 1, 3):
+                gout[l, d - 1] = dot(low, out_weight(l, ring(t, d))).astype(bf16)
+                put(gout.at[l, d - 1], gatt.at[l, own_rows(g)], *x_sems(4 * l + 1, g, d), along_x(d))
+            gatt[l, own_rows(g), :] = dot(low, weight(l, OUT0, UP0)).astype(bf16)
+            share_start(base + 1, ga.at[l], g)
+            note(5, dout)
+            note(1, g_gain)
+            note(3, g_shift)
+            note(4, low.astype(f32))
+        prepare(l)
         on_share()
-        share_wait(base + 1, ga.at[l])
-        attend_back(l, dot(ga[l], weight(l, OUT0, UP0)).astype(bf16), on_att)
-        part[5 + 2 * l] = dot_t(dqkv[l], weight(l, Q0, OUT0)).astype(bf16)
-        sum_start(base + 2, 5 + 2 * l)
+        drain()
+        for g in GROUPS:
+            for d in (1, 3, 2):
+                got(gatt.at[l, rows_of(g, ring(t, 4 - d))], *x_sems(4 * l + 1, g, d))
+        attend_back(l, gatt[l], on_att)
+        for g in GROUPS:
+            part[5 + 2 * l, group(g), :] = dot_t(dqkv[l, group(g), :], weight(l, Q0, OUT0)).astype(bf16)
+            sum_start(base + 2, 5 + 2 * l, g)
         keep_grad(l, Q0, dot(n1[l].T, dqkv[l]))
         scatter_a(l, "qkv")
         sums = jnp.sum(dqkv[l].astype(f32), axis=0, keepdims=True)
@@ -530,19 +646,24 @@
         two = jnp.where(((wide_col < 256) & (which == 0)) | ((wide_col >= 256) & (which == 1)), sums, 0.0)
         placed_rows = dot_t(two.astype(bf16), sel_ref[...])
         little[l, 7:9, :] = placed_rows[0:2]
+        for g in GROUPS:
+            share_wait(base + 1, ga.at[l], g)
         both[...] = dot(ga[l].T, att[l])
         on_last()
-        c = sum_wait(base + 2, 5 + 2 * l)
-        gv, g_gain, g_shift = norm_back(x_q, row[0:1], c)
-        little[l, 0:1, :] = g_gain
-        little[l, 2:3, :] = g_shift
-        return (gm + gv).astype(bf16)
+        drain()
+        for g in GROUPS:
+            c = sum_wait(base + 2, 5 + 2 * l, g)
+            gv, g_gain, g_shift = norm_back(x_ref[own_rows(g), :].astype(f32), row[0:1], c)
+            out_ref[own_rows(g), :] = (gmid[packed_rows(g), :] + gv).astype(bf16)
+            share_start(out_phase, out_ref, g)
+            note(0, g_gain)
+            note(2, g_shift)
 
     def out_grads(l):
         keep_grad(l, OUT0, jnp.concatenate([both[:, :128] + little[l].T, both[:, 128:]], axis=1))
 
 
-    A, B = 1, 0
+    B, U, V = 0, 1, 2
     gather_a(0, B)
     twin = ident(y, 3 - z, core, t)
     mine = pl.ds(pl.multiple_of(zh * BLOCK, BLOCK), BLOCK)
@@ -555,9 +676,12 @@
     x_all[mine, :] = f_ref[z, 0]
     g_all[mine, :] = og_ref[z, 0]
     gather_b(0, B)
-    gather_a(0, A)
+    gather_a(0, U)
+    gather_a(0, V)
     put(og_ref.at[3 - z, 0], g_all.at[mine], f_send.at[1], f_recv.at[1], twin)
     gather_c(0, B)
+    gather_b(0, U)
+    fetch_out(0)
     got(x_all.at[theirs], f_send.at[0], f_recv.at[0])
     gather_d(0, B)
     load_small(0)
@@ -569,66 +693,59 @@
 
         return body
 
-    def start_layer(l, ref):
-        n1[l] = norm(ref[...].astype(f32), small[l, 0:1, :], small[l, 2:3, :]).astype(bf16)
-        return ref[quarter, :].astype(f32)
-
-    x0 = start_layer(0, x_all)
-    x1_all[quarter, :] = forward(
-        0, x0,
-        run((gather_b, 0, A)),
-        run((gather_a, 1, B), (gather_a, 1, A)),
-        run((gather_c, 0, A)),
-        run((gather_b, 1, B)),
-    )
-    share_start(3, x1_all)
+    forward(
+        0, x_all, None, x1_all, 3,
+        run((pass_out, 0), (gather_c, 0, U), (gather_b, 0, V)),
+        run(),
+        run((gather_c, 0, V), (gather_a, 1, B), (gather_a, 1, U), (gather_a, 1, V)),
+        run((gather_b, 1, B), (gather_b, 1, U)),
+    )
     gather_c(1, B)
-    share_wait(3, x1_all)
     gather_d(1, B)
     load_small(1)
-    x1 = start_layer(1, x1_all)
-    o1_all[quarter, :] = forward(
-        1, x1, run((gather_b, 1, A)), run((place, 0, 0, x1_all)), run((gather_c, 1, A)), run()
+    forward(
+        1, x1_all, 3, o1_all, None,
+        run((pass_out, 1), (gather_c, 1, U), (gather_b, 1, V)), run(), run((gather_c, 1, V), (place, 0, 0, x1_all)),
+        run(),
     )
     got(g_all.at[theirs], f_send.at[1], f_recv.at[1])
-    gx1_all[quarter, :] = backward(
-        1, g_all[quarter, :].astype(f32), g_all, x1,
-        run((scatter_a, 1, "ud")), run((scatter_b, 1, "ud")), run((share_start, 7, o1_all)),
+    backward(
+        1, g_all, None, x1_all, gx1_all, 11,
+        run((scatter_a, 1, "ud")), run((scatter_b, 1, "ud")), run((share_all, 7, o1_all)),
         run((scatter_c, 1, "ud")),
     )
-    share_start(11, gx1_all)
     out_grads(1)
     scatter_a(1, "out")
     scatter_b(1, "qkv")
-    share_wait(11, gx1_all)
-    gx0_all[quarter, :] = backward(
-        0, gx1_all[quarter, :].astype(f32), gx1_all, x0,
+    backward(
+        0, gx1_all, 11, x_all, gx0_all, 15,
         run((scatter_a, 0, "ud"), (scatter_b, 1, "out")),
         run((scatter_b, 0, "ud")),
-        run((place, 1, 1, gx1_all), (share_wait, 7, o1_all), (place, 1, 0, o1_all)),
+        run((place, 1, 1, gx1_all), (shared_all, 7, o1_all), (place, 1, 0, o1_all)),
         run((scatter_c, 1, "qkv"), (scatter_c, 1, "out"), (scatter_c, 0, "ud"), (scatter_b, 0, "qkv")),
     )
     out_grads(0)
     scatter_a(0, "out")
-    share_start(15, gx0_all)
     for piece in ("ud", "qkv", "out"):
         scatter_d(1, piece)
     scatter_c(0, "qkv")
     scatter_b(0, "out")
     scatter_d(0, "ud")
-    share_wait(15, gx0_all)
+    shared_all(15, gx0_all)
     place(0, 1, gx0_all)
     scatter_c(0, "out")
     scatter_d(0, "qkv")
     scatter_d(0, "out")
     tiles[0] = own_ref[:, OUT0 : OUT0 + 128]
-    for d in (1, 2, 3):
+    for d in (1, 3, 2):
         put(tiles.at[0], tiles.at[d], t_send.at[d - 1], t_recv.at[d - 1], along_x(d))
     tile = tiles[0]
-    for d in (1, 2, 3):
+    for d in (1, 3, 2):
         got(tiles.at[d], t_send.at[d - 1], t_recv.at[d - 1])
         tile = tile + tiles[d]
-    tile_ref[...] = tile
+    column = lax.broadcasted_iota(jnp.int32, (SHARD, 128), 1)
+    turned[0:SHARD, :] = jnp.where(column < 6, tile, tiles[0])
+    small_ref[...] = turned[...].T[:16]
     for kind in range(2):
         for zz in range(4):
 
@@ -653,7 +770,7 @@
         layers_kernel,
         out_shape=(
             jax.ShapeDtypeStruct((SHARD, WIDE), f32),
-            jax.ShapeDtypeStruct((SHARD, 128), f32),
+            jax.ShapeDtypeStruct((16, 128), f32),
             jax.ShapeDtypeStruct((2, 4, BLOCK, D), bf16),
         ),
         in_specs=[vmem] * 9 + [pl.BlockSpec(memory_space=pltpu.SMEM)] + [vmem],
@@ -671,6 +788,13 @@
             pltpu.VMEM((ROWS, D), bf16),
             pltpu.VMEM((ROWS, D), bf16),
             pltpu.VMEM((D, 256), f32),
+            pltpu.VMEM((ROWS, D), bf16),
+            pltpu.VMEM((2, ROWS, 256), bf16),
+            pltpu.VMEM((2, 3, QUARTER, 256), bf16),
+            pltpu.VMEM((QUARTER, D), f32),
+            pltpu.VMEM((2, 4, 4, 2, 2, SHARD, UP0 - OUT0), bf16),
+            pltpu.VMEM((2, 4, ROWS, 256), bf16),
+            pltpu.VMEM((ROWS, D), f32),
             pltpu.VMEM((2, ROWS, D), bf16),
             pltpu.VMEM((2, ROWS, D), bf16),
             pltpu.VMEM((2, ROWS, D), bf16),
@@ -702,14 +826,15 @@
             pltpu.VMEM((3, SHARD, wide_a), bf16),
             pltpu.VMEM((3, SHARD, wide_b), bf16),
             pltpu.VMEM((4, SHARD, 128), f32),
-            dma((16, 3)), dma((16, 3)),
+            dma((16, 6)), dma((16, 6)),
+            dma((2, 11)), dma((2, 11)),
             dma((2, 7)), dma((2, 7)),
-            dma((2, 7)), dma((2, 7)),
-            dma((4, 7)), dma((4, 7)),
+            dma((6, 7)), dma((6, 7)),
             dma((6, 7)), dma((6, 7)),
             dma((2,)), dma((2,)),
             dma((4, 2)), dma((2, 4)), dma((2,)),
             dma((3,)), dma((3,)),
+            dma((2, 6)), dma((2, 6)),
         ],
         compiler_params=pltpu.CompilerParams(
             collective_id=0, has_side_effects=True, vmem_limit_bytes=VMEM_LIMIT
@@ -721,25 +846,23 @@
 def on_device(
     frames, w_qkv, w_out, w_up, w_down, ln_gains, shifts, qv_bias, up_bias, lengths, out_grad
 ):
-    own, tile, dist = layers_call(
+    own, little, outputs = layers_call(
         frames, jnp.transpose(w_qkv[0], (1, 0, 2)), w_out[0].T, w_up, w_down[0].T, ln_gains, shifts, qv_bias,
-        up_bias, lengths, out_grad,
-    )
-    outs = dist.astype(f32)
-    tile_t = tile.T
-    little_t = own[:, OUT0 : OUT0 + 64].T
+        up_bias, lengths.T, out_grad,
+    )
+    outputs = outputs.astype(f32)
     grad_qkv = jnp.stack([own[:, 0:192], own[:, 256:448], own[:, 448:640]], axis=1)
     return (
-        outs[0].reshape(1, 4, 1, BLOCK, D),
-        outs[1].reshape(1, 4, 1, BLOCK, D),
+        outputs[0].reshape(1, 4, 1, BLOCK, D),
+        outputs[1].reshape(1, 4, 1, BLOCK, D),
         grad_qkv[None],
         own[:, OUT0 + 64 : UP0].T[None],
         own[:, UP0:DOWN0][None],
         own[:, DOWN0:WIDE].T[None],
-        tile_t[0:2][None],
-        tile_t[2:6][None],
-        little_t[7:9, :12][None],
-        little_t[6:7],
+        little[None, 0:2, :SHARD],
+        little[None, 2:6, :SHARD],
+        little[None, 7:9, :12],
+        little[6:7, :SHARD],
     )
 
 

time: 203 us -> 198 us (0.975)
    unnamed x8 -> x5, local copies, waits for them, and re-layouts: 4.12 us -> 1.56 us
where the time goes in v4:
time: 198 us; the launch traced here: 196 us
  Pallas kernels  188 us (95%)
  local copies, waits for them, and re-layouts  5.21 us (3%)
  other arithmetic  2.14 us (1%)
    pallas_call x1, Pallas kernels, layers_call(): pl.pallas_call(layers_kernel, out_shape=(jax.ShapeDtypeStruct((SHARD, WID...  188 us

profile of v4, /device:TPU:1, one launch (start us, length us, event | category | flops | bytes accessed | tf_op | source)
XLA Modules:
  0.0 195.9 jit_solution(11342262608355856549)
XLA Ops:
  0.6 187.9 %layers.1 = (f32[48,2432]{1,0:T(8,128)}, f32[16,128]{1,0:T(8,128)}, bf16[2,4,96,768]{3,2,1,0:T(8,128)(2,1)}) custom-call(bf16[4,1,96,768]{3,2,1,0:T(8,128)(2,1)} %f_ref.1, bf16[3,48,192]{2,1,0:T(8,128)(2,1)} %bitcast.42, bf16[48,192]{1,0:T(8,128)(2,1)} %bitcast.44, bf16[1,48,768]{2,1,0:T(8,128)(2,1)} %wup_ref.1, bf16[48,768]{1,0:T(8,128)(2,1)} %bitcast.43, ...), custom_call_target="tpu_custom_call" | custom-call | tf_op jit(solution)/shard_map/layers/pallas_call | solution.py:769
  188.5 1.5 convert_element_type.3
  190.0 0.0 copy-start
  190.0 1.6 slice_bitcast_fusion
  191.6 0.0 copy-start.1
  191.6 0.0 copy-done
  191.6 0.7 slice_bitcast_fusion.4
  192.3 0.7 maximum_bitcast_fusion
  193.0 0.7 slice_bitcast_fusion.2
  193.7 0.0 copy-done.1
  193.7 0.6 slice_bitcast_fusion.10
  194.2 0.6 slice_bitcast_fusion.8
  194.8 0.6 slice_bitcast_fusion.9
  195.4 0.5 slice.47
Async XLA Ops:
  190.0 1.6 copy-start
  191.6 2.1 %copy-start.1 = (f32[16,128]{1,0:T(8,128)S(1)}, f32[16,128]{1,0:T(8,128)}, u32[]{:S(2)}) copy-start(f32[16,128]{1,0:T(8,128)} %get-tuple-element.15) | copy-start | bytes 24580
